TPU v7x, 32 devices: a whole 2x2x4 slice. The times are simulated.
32 devices in a mesh: groups: 2 (over y), docs: 8 (over z, x), help: 2 (over core).
Axes of the slice: x: 2, y: 2, z: 4, core: 2. Of those that a mesh axis runs over, the one named last changes fastest.
Arguments:
- token_states: bfloat16 [4096, 2, 1024], P(('groups', 'docs', 'help')), parts along dimension 0, may hold values from -6 to 6
- lengths: int32 [4096], P(('groups', 'docs', 'help')), parts along dimension 0, may hold values from 1 to 2
- cluster_id: int32 [4096], P(('groups', 'docs', 'help')), parts along dimension 0, may hold values from 0 to 7, as said below
- proj_weight: bfloat16 [1024, 1024], replicated, may hold values from -0.1875 to 0.1875
- proj_bias: float32 [1024], replicated, may hold values from -4 to 4
Outputs:
- max_sim: float32 [4096], P(('groups', 'docs', 'help')), parts along dimension 0
There are 2 independent parts, one for each index of `groups`. A program takes and returns all parts, laid end to end along the dimension named above; an argument that names none is the same for every part. Nothing has to cross between parts.
Inputs may be any that keep to these rules, and one draw needn't show every extreme that they name: `cluster_id`: clusters 1 * k to 1 * k + 1 - 1 form owner k. Among the 128 documents of one device (aligned blocks of the document dimension), at most 32 belong to one owner, and in every draw one owner gets exactly 32 documents from every device.
All inputs are finite; a program needn't handle non-finite values.
Results may differ from a plain program's by a relative error of at most 0.0003.
Values may be sent and summed in bfloat16 or wider, within the bound.
No kernel may reach another device: no remote copies, remote signals or barrier semaphores. Data moves between devices by JAX's collectives and lax.ppermute only.
A program may use at most 64 MiB of HBM per device.

v0:
```python
import jax
import jax.numpy as jnp
from jax import lax
from jax.sharding import PartitionSpec as P

CL_OWN = 1


def partner(value, axis, bit):
    return lax.ppermute(value, axis, [(i, i ^ 1 << bit) for i in range(lax.axis_size(axis))])


def slot_maxima(own_emb, own_ids, self_pos, col_emb, col_ids):
    row_total = own_emb.shape[0]
    block = min(row_total, 512)
    col_pos = lax.broadcasted_iota(jnp.int32, (col_emb.shape[0],), 0)

    def block_max(pieces):
        part_emb, part_ids, part_self = pieces
        duplicate_scores = jnp.einsum(
            "rd,cd->rc", part_emb, col_emb, preferred_element_type=jnp.float32
        )
        match = (
            (part_ids[:, None] == col_ids[None, :])
            & (col_ids[None, :] >= 0)
            & (part_self[:, None] != col_pos[None, :])
        )
        return jnp.max(jnp.where(match, duplicate_scores, -1.0), axis=1)

    steps_count = row_total // block
    result = lax.map(
        block_max,
        (
            own_emb.reshape(steps_count, block, own_emb.shape[1]),
            own_ids.reshape(steps_count, block),
            self_pos.reshape(steps_count, block),
        ),
    )
    return result.reshape(row_total)


def body(token_states, lengths, cluster_id, proj_weight, proj_bias):
    row_count, seq_len, feat_dim = token_states.shape
    owners = lax.axis_size("docs")
    slot_cap = 2 * row_count // owners
    position_count = owners * slot_cap
    token_mask = (
        lax.broadcasted_iota(jnp.int32, (row_count, seq_len), 1) < lengths[:, None]
    ).astype(jnp.bfloat16)
    summed = jnp.einsum("rsd,rs->rd", token_states, token_mask, preferred_element_type=jnp.float32)
    pooled = (summed / lengths[:, None].astype(jnp.float32)).astype(jnp.bfloat16)
    hidden = jnp.tanh(jnp.dot(pooled, proj_weight, preferred_element_type=jnp.float32) + proj_bias)
    factor = lax.rsqrt(jnp.sum(hidden * hidden, axis=1, keepdims=True) + 1e-06)
    embedded = (hidden * factor).astype(jnp.bfloat16)
    dest_owner = cluster_id // CL_OWN
    same_owner = dest_owner[:, None] == dest_owner[None, :]
    earlier = lax.broadcasted_iota(jnp.int32, (row_count, row_count), 1) < lax.broadcasted_iota(
        jnp.int32, (row_count, row_count), 0
    )
    slot_rank = jnp.sum((same_owner & earlier).astype(jnp.int32), axis=1)
    target = dest_owner * slot_cap + slot_rank
    chooser = lax.broadcasted_iota(jnp.int32, (position_count, row_count), 0) == target[None, :]
    packed = jnp.dot(
        chooser.astype(jnp.bfloat16), embedded, preferred_element_type=jnp.float32
    ).astype(jnp.bfloat16)
    packed_ids = jnp.max(jnp.where(chooser, cluster_id[None, :], -1), axis=1)
    own_emb, own_ids = (
        lax.all_to_all(packed, "docs", split_axis=0, concat_axis=0, tiled=True),
        lax.all_to_all(packed_ids, "docs", split_axis=0, concat_axis=0, tiled=True),
    )
    mate_emb, mate_ids = partner((own_emb, own_ids), "help", 0)
    col_emb = jnp.concatenate([own_emb, mate_emb], axis=0)
    col_ids = jnp.concatenate([own_ids, mate_ids], axis=0)
    self_pos = lax.broadcasted_iota(jnp.int32, (position_count,), 0)
    maxima = slot_maxima(own_emb, own_ids, self_pos, col_emb, col_ids)
    returned = lax.all_to_all(maxima, "docs", split_axis=0, concat_axis=0, tiled=True)
    return jnp.max(jnp.where(chooser, returned[:, None], -3.0), axis=0)


def solution(mesh):
    in_specs = (
        P(("groups", "docs", "help"), None, None),
        P(("groups", "docs", "help")),
        P(("groups", "docs", "help")),
        P(),
        P(),
    )
    out_specs = P(("groups", "docs", "help"))
    return jax.shard_map(body, mesh=mesh, in_specs=in_specs, out_specs=out_specs, check_vma=False)
```

profile of v0, /device:TPU:0, one launch (start us, length us, event | category | flops | bytes accessed | tf_op | source)
XLA Modules:
  0.0 52.1 jit_solution(1633893404897580692)
XLA Ops:
  0.0 0.9 %fusion.14 = pred[128,2,1]{1,0,2:T(32,128)(4,1)S(1)} fusion(s32[128]{0:T(128)} %param.6), kind=kLoop, calls=%fused_computation.26 | loop fusion | flops 256 | bytes 768 | tf_op jit(solution)/shard_map/lt | solution.py:48
  0.9 0.7 %convert_element_type.19 = f32[128]{0:T(128)S(1)} convert(s32[128]{0:T(128)} %param.6) | non-fusion elementwise | flops 128 | bytes 1024 | tf_op jit(solution)/shard_map/convert_element_type | solution.py:51
  1.6 0.9 %convert_reduce_fusion = s32[128]{0:T(128)S(1)} fusion(s32[128]{0:T(128)} %param.7), kind=kLoop, calls=%fused_computation.23 | loop fusion | flops 81792 | bytes 1024 | tf_op jit(solution)/shard_map/reduce_sum | solution.py:60
  2.5 0.7 %multiply_add_fusion = s32[128]{0:T(128)S(1)} fusion(s32[128]{0:T(128)S(1)} %convert_reduce_fusion, s32[128]{0:T(128)} %param.7), kind=kLoop, calls=%fused_computation.31 | loop fusion | flops 256 | bytes 1536 | tf_op jit(solution)/shard_map/add | solution.py:61
  3.1 1.7 %fusion.10 = f32[128,1,1024]{2,1,0:T(1,128)S(1)} fusion(bf16[128,2,1024]{2,1,0:T(2,128)(2,1)} %param.5, pred[128,2,1]{1,0,2:T(32,128)(4,1)S(1)} %fusion.14), kind=kOutput, calls=%fused_computation.16 | convolution fusion | flops 524288 | bytes 1048832 | tf_op jit(solution)/shard_map/rsd,rs->rd/dot_general | solution.py:50
  4.9 0.6 %multiply_reduce_fusion = (f32[128]{0:T(128)S(1)}, f32[128,1024]{1,0:T(8,128)S(1)}) fusion(f32[1024]{0:T(1024)S(1)} %copy-done.2, bf16[1024,1024]{1,0:T(8,128)(2,1)S(1)} %copy-done, f32[128,1,1024]{2,1,0:T(1,128)S(1)} %fusion.10, f32[128]{0:T(128)S(1)} %convert_element_type.19), kind=kOutput, calls=%fused_computation.11 | convolution fusion | flops 269090688 | bytes 3150848 | tf_op jit(solution)/shard_map/dot_general | solution.py:52
  5.5 0.4 convolution_convert_fusion
  5.9 21.6 %all_to_all.30 = bf16[8,32,1024]{2,1,0:T(8,128)(2,1)S(1)} all-to-all(bf16[8,32,1024]{2,1,0:T(8,128)(2,1)S(1)} %bitcast.18), channel_id=1, replica_groups=mesh['groups'=2,'docs'=8,'help'=2] {'docs'}, dimensions={0} | all-to-all | bytes 1048576 | tf_op jit(solution)/shard_map/all_to_all | solution.py:68
  27.4 0.1 select_reduce_fusion.2
  27.6 0.7 %all_to_all.20 = s32[8,32,1]{1,0,2:T(8,128)} reshape(s32[256]{0:T(256)S(1)} %select_reduce_fusion.2) | data formatting | bytes 2048 | tf_op jit(solution)/shard_map/all_to_all | solution.py:69
  28.2 3.6 %all-to-all-start = ((s32[8,32,1]{1,2,0:T(1,128)}), s32[8,32,1]{1,2,0:T(1,128)S(1)}, u32[]{:S(2)}, u32[]{:S(2)}) async-start(s32[8,32,1]{1,2,0:T(1,128)} %bitcast), calls=%async_computation | async-start | bytes 8192 | tf_op jit(solution)/shard_map/all_to_all | solution.py:69
  31.8 6.5 %all-to-all-done = s32[8,32,1]{1,2,0:T(1,128)S(1)} async-done(((s32[8,32,1]{1,2,0:T(1,128)}), s32[8,32,1]{1,2,0:T(1,128)S(1)}, u32[]{:S(2)}, u32[]{:S(2)}) %all-to-all-start) | async-done | bytes 1056 | tf_op jit(solution)/shard_map/all_to_all | solution.py:69
  38.3 0.5 broadcast.36
  38.8 0.7 %reduce.6 = s32[8,32]{1,0:T(8,128)S(1)} reduce(s32[8,32,1]{1,2,0:T(1,128)S(1)} %all-to-all-done, s32[]{:T(128)} %broadcast.36), dimensions={2}, to_apply=%all_to_all.21.reduce_sub_computation.3 | reduce | bytes 2052 | tf_op jit(solution)/shard_map/all_to_all | solution.py:69
  39.5 0.1 eq.48
  39.6 0.0 collective-permute-start
  39.6 1.1 %collective-permute-done = s32[256]{0:T(256)S(1)} collective-permute-done((s32[256]{0:T(256)S(1)}, s32[256]{0:T(256)S(1)}, u32[]{:S(2)}, u32[]{:S(2)}) %collective-permute-start) | collective-permute-done | bytes 1056 | tf_op jit(solution)/shard_map/ppermute | solution.py:10
  40.7 0.6 %select_reduce_fusion = f32[256]{0:T(256)S(1)} fusion(s32[512]{0:T(512)S(1)} %constant_dynamic-update-slice_fusion, s32[256]{0:T(256)S(1)} %eq.48, pred[512]{0:T(512)(128)(4,1)S(1)} %broadcast_compare_fusion, bf16[256,1024]{1,0:T(8,128)(2,1)S(1)} %bitcast.20, bf16[256,1024]{1,0:T(8,128)(2,1)S(1)} %collective-permute-done.1), kind=kOutput, calls=%fused_computation.9 | convolution fusion | flops 271318784 | bytes 1053184 | tf_op jit(solution)/shard_map/while/body/eval_jaxpr/rd,cd->rc/dot_general | solution.py:20
  41.3 0.1 all_to_all.25
  41.4 8.8 %all_to_all.31 = f32[8,32,1]{1,2,0:T(1,128)S(1)} all-to-all(f32[8,32,1]{1,2,0:T(1,128)S(1)} %bitcast.21), channel_id=1, replica_groups=mesh['groups'=2,'docs'=8,'help'=2] {'docs'}, dimensions={0} | all-to-all | bytes 2048 | tf_op jit(solution)/shard_map/all_to_all | solution.py:76
  50.2 0.5 broadcast.37
  50.7 0.7 %reduce.7 = f32[8,32]{1,0:T(8,128)S(1)} reduce(f32[8,32,1]{1,2,0:T(1,128)S(1)} %all_to_all.31, f32[]{:T(128)} %broadcast.37), dimensions={2}, to_apply=%all_to_all.26.reduce_sub_computation.3 | reduce | bytes 2052 | tf_op jit(solution)/shard_map/all_to_all | solution.py:76
  51.4 0.1 broadcast_in_dim.56
  51.5 0.6 %select_reduce_fusion.1 = f32[128]{0:T(128)} fusion(f32[256]{0:T(256)S(1)} %broadcast_in_dim.56, s32[128]{0:T(128)S(1)} %multiply_add_fusion), kind=kLoop, calls=%fused_computation.18 | loop fusion | flops 98176 | bytes 2048 | tf_op jit(solution)/shard_map/reduce_max | solution.py:77
  (13 shorter events, 0.1 us)
Async XLA Ops:
  0.0 4.9 %copy-start = (bf16[1024,1024]{1,0:T(8,128)(2,1)S(1)}, bf16[1024,1024]{1,0:T(8,128)(2,1)}, u32[]{:S(2)}) copy-start(bf16[1024,1024]{1,0:T(8,128)(2,1)} %param.8) | copy-start | bytes 6291460
  0.0 4.9 %copy-start.2 = (f32[1024]{0:T(1024)S(1)}, f32[1024]{0:T(1024)}, u32[]{:S(2)}) copy-start(f32[1024]{0:T(1024)} %param.9) | copy-start | bytes 12292
  5.5 22.0 %copy-start.1 = (s32[128]{0:T(128)S(1)}, s32[128]{0:T(128)}, u32[]{:S(2)}) copy-start(s32[128]{0:T(128)} %param.7) | copy-start | bytes 1540
  27.4 13.3 %collective-permute-start.1 = (bf16[256,1024]{1,0:T(8,128)(2,1)S(1)}, bf16[256,1024]{1,0:T(8,128)(2,1)S(1)}, u32[]{:S(2)}, u32[]{:S(2)}) collective-permute-start(bf16[256,1024]{1,0:T(8,128)(2,1)S(1)} %bitcast.19), channel_id=1, source_target_pairs={{0,1},{1,0},{2,3},{3,2},{4,5},{5,4},{6,7},{7,6},{8,9},{9,8},{10,11... | collective-permute-start | bytes 1572872 | tf_op jit(solution)/shard_map/ppermute | solution.py:10
  28.2 10.1 %all-to-all-start = ((s32[8,32,1]{1,2,0:T(1,128)}), s32[8,32,1]{1,2,0:T(1,128)S(1)}, u32[]{:S(2)}, u32[]{:S(2)}) async-start(s32[8,32,1]{1,2,0:T(1,128)} %bitcast), calls=%async_computation | async-start | bytes 8192 | tf_op jit(solution)/shard_map/all_to_all | solution.py:69
  39.6 1.1 %collective-permute-start = (s32[256]{0:T(256)S(1)}, s32[256]{0:T(256)S(1)}, u32[]{:S(2)}, u32[]{:S(2)}) collective-permute-start(s32[256]{0:T(256)S(1)} %eq.48), channel_id=1, source_target_pairs={{0,1},{1,0},{2,3},{3,2},{4,5},{5,4},{6,7},{7,6},{8,9},{9,8},{10,11... | collective-permute-start | bytes 3080 | tf_op jit(solution)/shard_map/ppermute | solution.py:10
where the time goes:
time: 52.4 us; the launch traced here: 52.1 us
  blocking collectives  30.4 us (58%)
  waiting for transfers between devices  7.58 us (14%)
  other arithmetic  5.19 us (10%)
  starting transfers between devices  3.6 us (7%)
  matrix products  3.24 us (6%)
  local copies, waits for them, and re-layouts  1.97 us (4%)
    all_to_all x1, blocking collectives, body(): lax.all_to_all(packed, 'docs', split_axis=0, concat_axis=0, tiled=True)  21.6 us
    all_to_all x1, blocking collectives, body(): lax.all_to_all(maxima, 'docs', split_axis=0, concat_axis=0, tiled=True)  8.82 us
    all_to_all x1, waiting for transfers between devices, body(): lax.all_to_all(packed_ids, 'docs', split_axis=0, concat_axis=0, tiled=True)  6.46 us
    all_to_all x1, starting transfers between devices, body(): lax.all_to_all(packed_ids, 'docs', split_axis=0, concat_axis=0, tiled=True)  3.59 us
    dot_general x1, matrix products, body(): jnp.einsum('rsd,rs->rd', token_states, token_mask, preferred_element_type...  1.73 us
    all_to_all x2, local copies, waits for them, and re-layouts, body(): lax.all_to_all(packed_ids, 'docs', split_axis=0, concat_axis=0, tiled=True)  1.19 us
    ppermute x2, waiting for transfers between devices, partner(): lax.ppermute(value, axis, [(i, i ^ 1 << bit) for i in range(lax.axis_size...  1.11 us
  transfers between devices with their start and end apart: 3, of which 2 were waited for; matrix products, arithmetic and copies ran while one was open for 3% of the time, Pallas kernels for 0%

commit v1 on v0

v1 whole, which is shorter than its diff:
```python
import functools

import jax
import jax.numpy as jnp
from jax import lax
from jax.experimental import pallas as pl
from jax.experimental.pallas import tpu as pltpu
from jax.sharding import PartitionSpec as P

CL_OWN = 1
LANES = 128
EMPTY = 2.0
VMEM = pl.BlockSpec(memory_space=pltpu.VMEM)
HBM = pl.BlockSpec(memory_space=pltpu.HBM)
PARAMS = pltpu.CompilerParams(vmem_limit_bytes=32 * 2**20)


def iota(shape, dim):
    return lax.broadcasted_iota(jnp.int32, shape, dim)


def in_hbm(array):
    return pltpu.with_memory_space_constraint(array, pltpu.HBM)


def embed_kernel(
    slot_cap, tok_hbm, len_hbm, id_hbm, weight_hbm, bias_hbm,
    packed_ref, place_ref,
    tok, weight, bias, lens, ids, sems,
):
    rows, seq_len, _ = tok.shape
    slots = packed_ref.shape[0]
    pairs = ((len_hbm, lens), (id_hbm, ids), (tok_hbm, tok), (weight_hbm, weight), (bias_hbm, bias))
    copies = [
        pltpu.make_async_copy(source, target, sems.at[at])
        for at, (source, target) in enumerate(pairs)
    ]
    for copy in copies:
        copy.start()
    diagonal = iota((rows, rows), 0) == iota((rows, rows), 1)

    def column(row):
        return jnp.sum(jnp.where(diagonal, row, 0), axis=1, keepdims=True)

    copies[0].wait()
    copies[1].wait()
    counts = column(lens[...])
    owner = ids[...] // CL_OWN
    earlier = (column(owner) == owner) & (iota((rows, rows), 0) < iota((rows, rows), 1))
    rank = jnp.sum(earlier.astype(jnp.int32), axis=0, keepdims=True)
    place_ref[0:1, :] = owner
    place_ref[1:2, :] = rank
    chooser = iota((slots, rows), 0) == owner * slot_cap + rank
    chooser = jnp.where(chooser, 1.0, 0.0)
    empty = jnp.sum(chooser, axis=1, keepdims=True) < 0.5
    copies[2].wait()
    summed = tok[:, 0, :].astype(jnp.float32)
    for t in range(1, seq_len):
        summed += jnp.where(counts > t, tok[:, t, :].astype(jnp.float32), 0.0)
    pooled = (summed / counts.astype(jnp.float32)).astype(jnp.bfloat16)
    copies[3].wait()
    copies[4].wait()
    hidden = jnp.tanh(
        jnp.dot(pooled, weight[...], preferred_element_type=jnp.float32) + bias[...]
    )
    factor = lax.rsqrt(jnp.sum(hidden * hidden, axis=1, keepdims=True) + 1e-06)
    embedded = (hidden * factor).astype(jnp.bfloat16)
    packed = jnp.dot(chooser.astype(jnp.bfloat16), embedded, preferred_element_type=jnp.float32)
    packed_ref[...] = packed.astype(jnp.bfloat16)
    first = packed_ref[:, 0:LANES].astype(jnp.float32)
    first = jnp.where(empty & (iota(first.shape, 1) == 0), EMPTY, first)
    packed_ref[:, 0:LANES] = first.astype(jnp.bfloat16)


def embed(token_states, lengths, cluster_id, proj_weight, proj_bias, owners):
    rows, _, width = token_states.shape
    slot_cap = 2 * rows // owners
    return pl.pallas_call(
        functools.partial(embed_kernel, slot_cap),
        out_shape=(
            jax.ShapeDtypeStruct((owners * slot_cap, width), jnp.bfloat16),
            jax.ShapeDtypeStruct((8, rows), jnp.int32),
        ),
        in_specs=[HBM] * 5,
        out_specs=(VMEM, VMEM),
        scratch_shapes=[
            pltpu.VMEM(token_states.shape, token_states.dtype),
            pltpu.VMEM(proj_weight.shape, proj_weight.dtype),
            pltpu.VMEM((1, width), jnp.float32),
            pltpu.VMEM((1, rows), jnp.int32),
            pltpu.VMEM((1, rows), jnp.int32),
            pltpu.SemaphoreType.DMA((5,)),
        ],
        compiler_params=PARAMS,
        name="embed",
    )(
        in_hbm(token_states),
        in_hbm(lengths.reshape(1, rows)),
        in_hbm(cluster_id.reshape(1, rows)),
        in_hbm(proj_weight),
        in_hbm(proj_bias.reshape(1, width)),
    )


def score_kernel(slot_cap, own_ref, mate_ref, out_ref):
    own = own_ref[...]
    slots = own.shape[0]

    def best(ref, mine):
        scores = lax.dot_general(
            ref[...], own, (((1,), (1,)), ((), ())), preferred_element_type=jnp.float32
        )
        valid = ref[:, 0:LANES][:, 0:1].astype(jnp.float32) < 1.5
        if mine:
            valid = valid & (iota((slots, slots), 0) != iota((slots, slots), 1))
        return jnp.max(jnp.where(valid, scores, -1.0), axis=0, keepdims=True)

    maxima = jnp.maximum(best(own_ref, True), best(mate_ref, False))
    for source in range(slots // slot_cap):
        out_ref[source, :, 0:slot_cap] = maxima[:, source * slot_cap : (source + 1) * slot_cap]


def score(own, mate, owners):
    slot_cap = own.shape[0] // owners
    lanes = -(-slot_cap // LANES) * LANES
    return pl.pallas_call(
        functools.partial(score_kernel, slot_cap),
        out_shape=jax.ShapeDtypeStruct((owners, 1, lanes), jnp.float32),
        in_specs=[VMEM, VMEM],
        out_specs=VMEM,
        compiler_params=PARAMS,
        name="score",
    )(own, mate)


def pick_kernel(returned_ref, place_ref, out_ref):
    owners, _, lanes = returned_ref.shape
    rows = place_ref.shape[1]
    owner = place_ref[0:1, :]
    rank = jnp.broadcast_to(place_ref[1:2, :], (owners, rows))
    returned = returned_ref[...].reshape(owners, lanes)
    taken = jnp.take_along_axis(returned, rank, axis=1, mode="promise_in_bounds")
    taken = jnp.where(iota((owners, rows), 0) == owner, taken, -3.0)
    out_ref[...] = jnp.max(taken, axis=0, keepdims=True)


def pick(returned, place):
    rows = place.shape[1]
    return pl.pallas_call(
        pick_kernel,
        out_shape=jax.ShapeDtypeStruct((1, rows), jnp.float32),
        in_specs=[VMEM, VMEM],
        out_specs=VMEM,
        name="pick",
    )(returned, place).reshape(rows)


def body(token_states, lengths, cluster_id, proj_weight, proj_bias):
    owners = lax.axis_size("docs")
    packed, place = embed(token_states, lengths, cluster_id, proj_weight, proj_bias, owners)
    own = lax.all_to_all(packed, "docs", split_axis=0, concat_axis=0, tiled=True)
    swap = [(i, i ^ 1) for i in range(lax.axis_size("help"))]
    mate = lax.ppermute(own, "help", swap)
    maxima = score(own, mate, owners)
    returned = lax.all_to_all(maxima, "docs", split_axis=0, concat_axis=0, tiled=True)
    return pick(returned, place)


def solution(mesh):
    spread = P(("groups", "docs", "help"))
    in_specs = (P(("groups", "docs", "help"), None, None), spread, spread, P(), P())
    return jax.shard_map(body, mesh=mesh, in_specs=in_specs, out_specs=spread, check_vma=False)
```

time: 52.4 us -> 38.2 us (0.73)
  waiting for transfers between devices: 7.58 us -> 1.9 us
  other arithmetic: 5.19 us -> 0 us
  Pallas kernels: 0 us -> 4.51 us
  starting transfers between devices: 3.6 us -> 0.01 us
  matrix products: 3.24 us -> 0 us
  local copies, waits for them, and re-layouts: 1.97 us -> 0.01 us
  blocking collectives: 30.4 us -> 31.5 us
    all_to_all x1 -> x0, waiting for transfers between devices: 6.46 us -> none  [body(): lax.all_to_all(packed_ids, 'docs', split_axis=0, concat_axis=0, tiled=True)]
    pallas_call x0 -> x3, Pallas kernels: none -> 4.51 us  [the longest x1 2.69 us: embed(): pl.pallas_call(functools.partial(embed_kernel, slot_cap), out_shape=(jax....]
    all_to_all x1 -> x0, starting transfers between devices: 3.59 us -> none  [body(): lax.all_to_all(packed_ids, 'docs', split_axis=0, concat_axis=0, tiled=True)]
    dot_general x4 -> x0, matrix products: 3.24 us -> none  [the longest x1 1.73 us: body(): jnp.einsum('rsd,rs->rd', token_states, token_mask, preferred_element_type...]
    all_to_all x4 -> x0, local copies, waits for them, and re-layouts: 1.78 us -> none  [the longest x2 1.19 us: body(): lax.all_to_all(packed_ids, 'docs', split_axis=0, concat_axis=0, tiled=True)]
    all_to_all x2 -> x0, other arithmetic: 1.32 us -> none  [the longest x1 0.66 us: body(): lax.all_to_all(packed_ids, 'docs', split_axis=0, concat_axis=0, tiled=True)]
    all_to_all x1, blocking collectives: 8.82 us -> 9.95 us  [body(): lax.all_to_all(maxima, 'docs', split_axis=0, concat_axis=0, tiled=True)]
    reduce_sum x1 -> x0, other arithmetic: 0.9 us -> none  [body(): slot_rank = jnp.sum((same_owner & earlier).astype(jnp.int32), axis=1)]
  transfers between devices with their start and end apart: 3 -> 1, of which waited for: 2 -> 1; matrix products, arithmetic and copies ran while one was open for 3% -> 0% of each run, Pallas kernels for 0% -> 0%
where the time goes in v1:
time: 38.2 us; the launch traced here: 38 us
  blocking collectives  31.5 us (82%)
  Pallas kernels  4.51 us (12%)
  waiting for transfers between devices  1.9 us (5%)
    all_to_all x1, blocking collectives, body(): lax.all_to_all(packed, 'docs', split_axis=0, concat_axis=0, tiled=True)  21.6 us
    all_to_all x1, blocking collectives, body(): lax.all_to_all(maxima, 'docs', split_axis=0, concat_axis=0, tiled=True)  9.95 us
    pallas_call x1, Pallas kernels, embed(): pl.pallas_call(functools.partial(embed_kernel, slot_cap), out_shape=(jax....  2.69 us
    ppermute x1, waiting for transfers between devices, body(): mate = lax.ppermute(own, 'help', swap)  1.9 us
    pallas_call x1, Pallas kernels, pick(): pl.pallas_call(pick_kernel, out_shape=jax.ShapeDtypeStruct((1, rows), jnp...  1.27 us
  transfers between devices with their start and end apart: 1, of which 1 were waited for; matrix products, arithmetic and copies ran while one was open for 0% of the time, Pallas kernels for 0%

profile of v1, /device:TPU:0, one launch (start us, length us, event | category | flops | bytes accessed | tf_op | source)
XLA Modules:
  0.0 38.0 jit_solution(2900672404910257989)
XLA Ops:
  0.0 2.7 %embed.1 = (bf16[256,1024]{1,0:T(8,128)(2,1)S(1)}, s32[8,128]{1,0:T(8,128)S(1)}) custom-call(bf16[128,2,1024]{2,1,0:T(2,128)(2,1)} %tok_hbm.1, s32[1,128]{1,0:T(1,128)} %bitcast.10, s32[1,128]{1,0:T(1,128)} %bitcast.11, bf16[1024,1024]{1,0:T(8,128)(2,1)} %weight_hbm.1, f32[1,1024]{1,0:T(1,128)} %bitcast.9), custom_call_target="tpu_custom_call" | custom-call | tf_op jit(solution)/shard_map/embed/pallas_call | solution.py:78
  2.7 0.0 copy-start
  2.7 21.6 %all_to_all.16 = bf16[8,32,1024]{2,1,0:T(8,128)(2,1)S(1)} all-to-all(bf16[8,32,1024]{2,1,0:T(8,128)(2,1)S(1)} %bitcast.8), channel_id=1, replica_groups=mesh['groups'=2,'docs'=8,'help'=2] {'docs'}, dimensions={0} | all-to-all | bytes 1048576 | tf_op jit(solution)/shard_map/all_to_all | solution.py:161
  24.3 0.0 collective-permute-start
  24.3 0.0 copy-done
  24.3 1.9 %collective-permute-done.mate_ref = bf16[256,1024]{1,0:T(8,128)(2,1)S(1)} collective-permute-done((bf16[256,1024]{1,0:T(8,128)(2,1)S(1)}, bf16[256,1024]{1,0:T(8,128)(2,1)S(1)}, u32[]{:S(2)}, u32[]{:S(2)}) %collective-permute-start) | collective-permute-done | bytes 524320 | tf_op jit(solution)/shard_map/ppermute | solution.py:163
  26.2 0.5 %score.1 = f32[8,1,128]{2,1,0:T(1,128)S(1)} custom-call(bf16[256,1024]{1,0:T(8,128)(2,1)S(1)} %bitcast.7, bf16[256,1024]{1,0:T(8,128)(2,1)S(1)} %collective-permute-done.mate_ref), custom_call_target="tpu_custom_call" | custom-call | tf_op jit(solution)/shard_map/score/pallas_call | solution.py:126
  26.7 10.0 %all_to_all.17.returned_ref = f32[8,1,128]{2,1,0:T(1,128)} all-to-all(f32[8,1,128]{2,1,0:T(1,128)S(1)} %score.1), channel_id=1, replica_groups=mesh['groups'=2,'docs'=8,'help'=2] {'docs'}, dimensions={0} | all-to-all | bytes 8192 | tf_op jit(solution)/shard_map/all_to_all | solution.py:165
  36.7 1.3 %pick.1 = f32[1,128]{1,0:T(1,128)} custom-call(f32[8,1,128]{2,1,0:T(1,128)} %all_to_all.17.returned_ref, s32[8,128]{1,0:T(8,128)} %copy-done), custom_call_target="tpu_custom_call" | custom-call | tf_op jit(solution)/shard_map/pick/pallas_call | solution.py:149
Async XLA Ops:
  2.7 21.6 %copy-start = (s32[8,128]{1,0:T(8,128)}, s32[8,128]{1,0:T(8,128)S(1)}, u32[]{:S(2)}) copy-start(s32[8,128]{1,0:T(8,128)S(1)} %get-tuple-element.8.place_ref) | copy-start | bytes 12292
  24.3 1.9 %collective-permute-start = (bf16[256,1024]{1,0:T(8,128)(2,1)S(1)}, bf16[256,1024]{1,0:T(8,128)(2,1)S(1)}, u32[]{:S(2)}, u32[]{:S(2)}) collective-permute-start(bf16[256,1024]{1,0:T(8,128)(2,1)S(1)} %bitcast.6), channel_id=1, source_target_pairs={{0,1},{1,0},{2,3},{3,2},{4,5},{5,4},{6,7},{7,6},{8,9},{9,8},{10,11... | collective-permute-start | bytes 1572872 | tf_op jit(solution)/shard_map/ppermute | solution.py:163

commit v2 on v1

v2 whole, which is shorter than its diff:
```python
import functools

import jax
import jax.numpy as jnp
from jax import lax
from jax.experimental import pallas as pl
from jax.experimental.pallas import tpu as pltpu
from jax.sharding import PartitionSpec as P

CL_OWN = 1
LANES = 128
EMPTY = 2.0
VMEM = pl.BlockSpec(memory_space=pltpu.VMEM)
SMEM = pl.BlockSpec(memory_space=pltpu.SMEM)
HBM = pl.BlockSpec(memory_space=pltpu.HBM)
PARAMS = pltpu.CompilerParams(vmem_limit_bytes=32 * 2**20)

PLAN = (("own", (6, 7)), ("own", (1, 1)), ("own", (7, 6)), ("own", (2, 3)), ("own", (4, 5)), ("own", (3, 2)), ("own", (5, 4)))
GROUPS = ((0,), (1,), (2,), (3,), (4,), (5,), (6,))
AFTER = {}


def iota(shape, dim):
    return lax.broadcasted_iota(jnp.int32, shape, dim)


def in_hbm(array):
    return pltpu.with_memory_space_constraint(array, pltpu.HBM)


def in_vmem(array):
    return pltpu.with_memory_space_constraint(array, pltpu.VMEM)


def rows_of(at, slot_cap, blocks=1):
    return pl.ds(at * slot_cap, blocks * slot_cap)


def layout(core):
    alone = [[steps[core]] for kind, steps in PLAN if kind == "own"]
    keep = [steps[core] for kind, steps in PLAN if kind == "both"]
    give = [steps[1 - core] for kind, steps in PLAN if kind != "own"] + [0]
    return [*alone, keep, give] if keep else [*alone, give]


def embed_kernel(
    slot_cap, block_of, me_ref, core_ref,
    tok_hbm, len_hbm, id_hbm, weight_hbm, bias_hbm, *refs,
):
    *packed_refs, place_ref, tok, weight, bias, lens, ids, sems = refs
    rows, seq_len, _ = tok.shape
    slots = sum(ref.shape[0] for ref in packed_refs)
    pairs = ((len_hbm, lens), (id_hbm, ids), (tok_hbm, tok), (weight_hbm, weight), (bias_hbm, bias))
    copies = [
        pltpu.make_async_copy(source, target, sems.at[at])
        for at, (source, target) in enumerate(pairs)
    ]
    for copy in copies:
        copy.start()
    diagonal = iota((rows, rows), 0) == iota((rows, rows), 1)

    def column(row):
        return jnp.sum(jnp.where(diagonal, row, 0), axis=1, keepdims=True)

    copies[0].wait()
    copies[1].wait()
    counts = column(lens[...])
    owner = ids[...] // CL_OWN
    earlier = (column(owner) == owner) & (iota((rows, rows), 0) < iota((rows, rows), 1))
    rank = jnp.sum(earlier.astype(jnp.int32), axis=0, keepdims=True)
    place_ref[0:1, :] = owner
    place_ref[1:2, :] = rank
    block = block_of(owner, me_ref, core_ref)
    chooser = iota((slots, rows), 0) == block * slot_cap + rank
    chooser = jnp.where(chooser, 1.0, 0.0)
    empty = jnp.sum(chooser, axis=1, keepdims=True) < 0.5
    copies[2].wait()
    summed = tok[:, 0, :].astype(jnp.float32)
    for t in range(1, seq_len):
        summed += jnp.where(counts > t, tok[:, t, :].astype(jnp.float32), 0.0)
    pooled = (summed / counts.astype(jnp.float32)).astype(jnp.bfloat16)
    copies[3].wait()
    copies[4].wait()
    hidden = jnp.tanh(
        jnp.dot(pooled, weight[...], preferred_element_type=jnp.float32) + bias[...]
    )
    factor = lax.rsqrt(jnp.sum(hidden * hidden, axis=1, keepdims=True) + 1e-06)
    embedded = (hidden * factor).astype(jnp.bfloat16)
    packed = jnp.dot(chooser.astype(jnp.bfloat16), embedded, preferred_element_type=jnp.float32)
    first = packed[:, 0:LANES]
    first = jnp.where(empty & (iota(first.shape, 1) == 0), EMPTY, first).astype(jnp.bfloat16)
    rest = packed[:, LANES:].astype(jnp.bfloat16)
    at = 0
    for ref in packed_refs:
        ref[:, 0:LANES] = first[at : at + ref.shape[0]]
        ref[:, LANES:] = rest[at : at + ref.shape[0]]
        at += ref.shape[0]


def plan_block(owner, me_ref, core_ref):
    step = owner ^ me_ref[0]
    block = jnp.zeros_like(step)
    flat = [sum(layout(core), []) for core in range(2)]
    for at in range(len(flat[0])):
        block = jnp.where(step == jnp.where(core_ref[0] == 0, flat[0][at], flat[1][at]), at, block)
    return block


def embed(me, core, arrays, sizes, slot_cap, block_of):
    token_states, lengths, cluster_id, proj_weight, proj_bias = arrays
    rows, _, width = token_states.shape
    return pl.pallas_call(
        functools.partial(embed_kernel, slot_cap, block_of),
        out_shape=[jax.ShapeDtypeStruct((size, width), jnp.bfloat16) for size in sizes]
        + [jax.ShapeDtypeStruct((8, rows), jnp.int32)],
        in_specs=[SMEM] * 2 + [HBM] * 5,
        out_specs=[VMEM] * (len(sizes) + 1),
        scratch_shapes=[
            pltpu.VMEM(token_states.shape, token_states.dtype),
            pltpu.VMEM(proj_weight.shape, proj_weight.dtype),
            pltpu.VMEM((1, width), jnp.float32),
            pltpu.VMEM((1, rows), jnp.int32),
            pltpu.VMEM((1, rows), jnp.int32),
            pltpu.SemaphoreType.DMA((5,)),
        ],
        compiler_params=PARAMS,
        name="embed",
    )(
        me,
        core,
        in_hbm(token_states),
        in_hbm(lengths.reshape(1, rows)),
        in_hbm(cluster_id.reshape(1, rows)),
        in_hbm(proj_weight),
        in_hbm(proj_bias.reshape(1, width)),
    )


def move_kernel(count, moves, core_ref, *refs):
    in_refs, out_refs = refs[:count], refs[len(refs) - len(moves[0]) :]
    for core in range(2):

        @pl.when(core_ref[0] == core)
        def _():
            for ref, parts in zip(out_refs, moves[core]):
                at = 0
                for source, part in parts:
                    size = part.size
                    ref[pl.ds(at, size), :] = in_refs[source][part, :]
                    at += size


def move(core, values, moves, name, after=()):
    width, kind = values[0].shape[1], values[0].dtype
    sizes = [sum(part.size for _, part in parts) for parts in moves[0]]
    return pl.pallas_call(
        functools.partial(move_kernel, len(values), moves),
        out_shape=[jax.ShapeDtypeStruct((size, width), kind) for size in sizes],
        in_specs=[SMEM] + [VMEM] * (len(values) + len(after)),
        out_specs=[VMEM] * len(sizes),
        compiler_params=PARAMS,
        name=name,
    )(core, *values, *after)


def best_of(ref, columns, same):
    scores = lax.dot_general(
        ref[...], columns, (((1,), (1,)), ((), ())), preferred_element_type=jnp.float32
    )
    valid = ref[:, 0:LANES].astype(jnp.float32)[:, 0:1] < 1.5
    if same:
        valid = valid & (iota(scores.shape, 0) != iota(scores.shape, 1))
    return jnp.max(jnp.where(valid, scores, -1.0), axis=0, keepdims=True)


def write_maxima(out_ref, mine, other, sources, slot_cap):
    columns = mine[...]
    maxima = jnp.maximum(best_of(mine, columns, True), best_of(other, columns, False))
    for at, source in enumerate(sources):
        out_ref[source, :, 0:slot_cap] = maxima[:, at * slot_cap : (at + 1) * slot_cap]


def score_kernel(slot_cap, me_ref, core_ref, give_ref, got_ref, *refs):
    *parts, out_ref, mine, other = refs
    received, handed = parts[: len(PLAN)], parts[len(PLAN) :]
    own = rows_of(give_ref.shape[0] // slot_cap - 1, slot_cap)
    places = [((0, 0), [((give_ref, own), (got_ref, own))] * 2)]
    offsets = {}
    for group, members in enumerate(GROUPS):
        at = 0
        for op in members:
            offsets[op] = (handed[group], at)
            at += 2 if PLAN[op][0] == "both" else 1
    for op, (kind, steps) in enumerate(PLAN):
        ours = (received[op], rows_of(0, slot_cap))
        theirs = (offsets[op][0], rows_of(offsets[op][1], slot_cap))
        if kind == "own":
            places.append((steps, [(ours, theirs)] * 2))
        elif kind == "mate":
            places.append((steps[::-1], [(theirs, ours)] * 2))
        else:
            for (ref, start), order in (((received[op], 0), steps), (offsets[op], steps[::-1])):
                pair = [(ref, rows_of(start + core, slot_cap)) for core in range(2)]
                places.append((order, [(pair[core], pair[1 - core]) for core in range(2)]))
    for core in range(2):

        @pl.when(core_ref[0] == core)
        def _():
            for at, (_, by_core) in enumerate(places):
                (ours, our_rows), (theirs, their_rows) = by_core[core]
                mine[rows_of(at, slot_cap), :] = ours[our_rows, :]
                other[rows_of(at, slot_cap), :] = theirs[their_rows, :]

    sources = [me_ref[0] ^ jnp.where(core_ref[0] == 0, *steps) for steps, _ in places]
    write_maxima(out_ref, mine, other, sources, slot_cap)


def score(me, core, give, got, parts, owners, slot_cap):
    width = give.shape[1]
    lanes = -(-slot_cap // LANES) * LANES
    return pl.pallas_call(
        functools.partial(score_kernel, slot_cap),
        out_shape=jax.ShapeDtypeStruct((owners, 1, lanes), jnp.float32),
        in_specs=[SMEM] * 2 + [VMEM] * (2 + len(parts)),
        out_specs=VMEM,
        scratch_shapes=[pltpu.VMEM((owners * slot_cap, width), give.dtype)] * 2,
        compiler_params=PARAMS,
        name="score",
    )(me, core, give, got, *parts)


def plain_score_kernel(slot_cap, mine_ref, other_ref, out_ref):
    write_maxima(out_ref, mine_ref, other_ref, range(out_ref.shape[0]), slot_cap)


def plain_score(mine, other, owners, slot_cap):
    lanes = -(-slot_cap // LANES) * LANES
    return pl.pallas_call(
        functools.partial(plain_score_kernel, slot_cap),
        out_shape=jax.ShapeDtypeStruct((owners, 1, lanes), jnp.float32),
        in_specs=[VMEM, VMEM],
        out_specs=VMEM,
        compiler_params=PARAMS,
        name="score",
    )(mine, other)


def pick_kernel(returned_ref, place_ref, out_ref):
    owners, _, lanes = returned_ref.shape
    rows = place_ref.shape[1]
    owner = place_ref[0:1, :]
    rank = jnp.broadcast_to(place_ref[1:2, :], (owners, rows))
    returned = returned_ref[...].reshape(owners, lanes)
    taken = jnp.take_along_axis(returned, rank, axis=1, mode="promise_in_bounds")
    taken = jnp.where(iota((owners, rows), 0) == owner, taken, -3.0)
    out_ref[...] = jnp.max(taken, axis=0, keepdims=True)


def pick(returned, place):
    rows = place.shape[1]
    return pl.pallas_call(
        pick_kernel,
        out_shape=jax.ShapeDtypeStruct((1, rows), jnp.float32),
        in_specs=[VMEM, VMEM],
        out_specs=VMEM,
        name="pick",
    )(in_vmem(returned), in_vmem(place)).reshape(rows)


def step_to(value, steps):
    helpers = lax.axis_size("help")
    pairs = [
        (doc * helpers + core, (doc ^ steps[core]) * helpers + core)
        for doc in range(lax.axis_size("docs"))
        for core in range(helpers)
    ]
    return lax.ppermute(value, ("docs", "help"), pairs)


def swap(value):
    return lax.ppermute(value, "help", [(i, i ^ 1) for i in range(lax.axis_size("help"))])


def planned_scores(me, core, arrays, owners, slot_cap):
    sizes = [len(steps) * slot_cap for steps in layout(0)]
    *packed, place = embed(me, core, arrays, sizes, slot_cap, plan_block)
    alone = iter(packed)
    give = packed[-1]
    keep = packed[-2]
    got = swap(give)
    merged, at_keep, at_got = {}, 0, 0
    wanted = {}
    for op, (kind, _) in enumerate(PLAN):
        wait = AFTER.get(op, ())
        if kind == "own":
            merged[op] = next(alone)
            if wait:
                wanted.setdefault(wait, []).append((op, "own", None, None))
            continue
        wanted.setdefault(wait, []).append((op, kind, at_keep, at_got))
        at_got += 1
        at_keep += kind == "both"
    received = {}

    def send(op):
        received[op] = step_to(merged[op], PLAN[op][1])

    for op in range(len(PLAN)):
        if PLAN[op][0] == "own" and not AFTER.get(op, ()):
            send(op)
    for wait, ops in wanted.items():
        values = [keep, got]
        moves = [[], []]
        for op, kind, from_keep, from_got in ops:
            if kind == "own":
                values.append(merged[op])
                for core_moves in moves:
                    core_moves.append([(len(values) - 1, rows_of(0, slot_cap))])
                continue
            theirs = (1, rows_of(from_got, slot_cap))
            if kind == "mate":
                for core_moves in moves:
                    core_moves.append([theirs])
                continue
            ours = (0, rows_of(from_keep, slot_cap))
            moves[0].append([ours, theirs])
            moves[1].append([theirs, ours])
        outs = move(core, values, moves, "merge", [received[op] for op in wait])
        for (op, *_), out in zip(ops, outs):
            merged[op] = out
            send(op)
    handed = []
    for members in GROUPS:
        values = [received[op] for op in members]
        if len(values) > 1:
            parts = [(at, pl.ds(0, value.shape[0])) for at, value in enumerate(values)]
            (joined,) = move(core, values, [[parts], [parts]], "join")
        else:
            joined = values[0]
        handed.append(swap(joined))
    parts = [received[op] for op in range(len(PLAN))] + handed
    return score(me, core, give, got, parts, owners, slot_cap), place


def plain_scores(me, core, arrays, owners, slot_cap):
    packed, place = embed(
        me, core, arrays, [owners * slot_cap], slot_cap, lambda owner, *_: owner
    )
    mine = lax.all_to_all(packed, "docs", split_axis=0, concat_axis=0, tiled=True)
    return plain_score(mine, swap(mine), owners, slot_cap), place


def body(*arrays):
    owners = lax.axis_size("docs")
    slot_cap = 2 * arrays[0].shape[0] // owners
    me = lax.axis_index("docs").reshape(1)
    core = lax.axis_index("help").reshape(1)
    planned = sum(len(steps) for steps in layout(0)) == owners
    scores = planned_scores if planned else plain_scores
    maxima, place = scores(me, core, arrays, owners, slot_cap)
    returned = lax.all_to_all(maxima, "docs", split_axis=0, concat_axis=0, tiled=True)
    return pick(returned, place)


def solution(mesh):
    spread = P(("groups", "docs", "help"))
    in_specs = (P(("groups", "docs", "help"), None, None), spread, spread, P(), P())
    return jax.shard_map(body, mesh=mesh, in_specs=in_specs, out_specs=spread, check_vma=False)
```

time: 38.2 us -> 34.3 us (0.90)
  blocking collectives: 31.5 us -> 10.2 us
  starting transfers between devices: 0.01 us -> 15 us
  waiting for transfers between devices: 1.9 us -> 4.9 us
  Pallas kernels: 4.51 us -> 3.88 us
    all_to_all x1 -> x0, blocking collectives: 21.6 us -> none  [body(): lax.all_to_all(packed, 'docs', split_axis=0, concat_axis=0, tiled=True)]
    ppermute x1 -> x15, starting transfers between devices: 0.01 us -> 15 us  [the longest x7 13.4 us: step_to(): return lax.ppermute(value, ('docs', 'help'), pairs)]
    ppermute x1 -> x15, waiting for transfers between devices: 1.9 us -> 4.9 us  [the longest x7 4 us: step_to(): return lax.ppermute(value, ('docs', 'help'), pairs)]
    pallas_call x1, Pallas kernels: 1.27 us -> 0.59 us  [pick(): pl.pallas_call(pick_kernel, out_shape=jax.ShapeDtypeStruct((1, rows), jnp...]
  transfers between devices with their start and end apart: 1 -> 15, of which waited for: 1 -> 7; matrix products, arithmetic and copies ran while one was open for 0% -> 0% of each run, Pallas kernels for 0% -> 0%
where the time goes in v2:
time: 34.3 us; the launch traced here: 34.1 us
  starting transfers between devices  15 us (44%)
  blocking collectives  10.2 us (30%)
  waiting for transfers between devices  4.9 us (14%)
  Pallas kernels  3.88 us (11%)
    ppermute x7, starting transfers between devices, step_to(): return lax.ppermute(value, ('docs', 'help'), pairs)  13.4 us
    all_to_all x1, blocking collectives, body(): lax.all_to_all(maxima, 'docs', split_axis=0, concat_axis=0, tiled=True)  10.2 us
    ppermute x7, waiting for transfers between devices, step_to(): return lax.ppermute(value, ('docs', 'help'), pairs)  4 us
    pallas_call x1, Pallas kernels, embed(): pl.pallas_call(functools.partial(embed_kernel, slot_cap, block_of), out_s...  2.66 us
    ppermute x8, starting transfers between devices, swap(): lax.ppermute(value, 'help', [(i, i ^ 1) for i in range(lax.axis_size('hel...  1.6 us
    ppermute x8, waiting for transfers between devices, swap(): lax.ppermute(value, 'help', [(i, i ^ 1) for i in range(lax.axis_size('hel...  0.91 us
  transfers between devices with their start and end apart: 15, of which 7 were waited for; matrix products, arithmetic and copies ran while one was open for 0% of the time, Pallas kernels for 0%

profile of v2, /device:TPU:0, one launch (start us, length us, event | category | flops | bytes accessed | tf_op | source)
XLA Modules:
  0.0 34.1 jit_solution(15231267496194727166)
XLA Ops:
  0.0 2.7 %embed.1 = (bf16[32,1024]{1,0:T(8,128)(2,1)S(1)}, bf16[32,1024]{1,0:T(8,128)(2,1)S(1)}, bf16[32,1024]{1,0:T(8,128)(2,1)S(1)}, bf16[32,1024]{1,0:T(8,128)(2,1)S(1...) custom-call(s32[1]{0:T(128)} %bitcast.me_ref, ...), custom_call_target="tpu_custom_call" | custom-call | tf_op jit(solution)/shard_map/embed/pallas_call | solution.py:112
  2.7 5.1 %collective-permute-start.1 = (bf16[32,1024]{1,0:T(8,128)(2,1)S(1)}, bf16[32,1024]{1,0:T(8,128)(2,1)S(1)}, u32[]{:S(2)}, u32[]{:S(2)}) collective-permute-start(bf16[32,1024]{1,0:T(8,128)(2,1)S(1)} %get-tuple-element.15), channel_id=1, source_target_pairs={{0,12},{1,15},{2,14},{3,13},{4,8},{5,11},{6,10},{7,9},{8,4},{9,7},... | collective-permute-start | bytes 196616 | tf_op jit(solution)/shard_map/ppermute | solution.py:277
  7.8 1.5 %collective-permute-start.2 = (bf16[32,1024]{1,0:T(8,128)(2,1)S(1)}, bf16[32,1024]{1,0:T(8,128)(2,1)S(1)}, u32[]{:S(2)}, u32[]{:S(2)}) collective-permute-start(bf16[32,1024]{1,0:T(8,128)(2,1)S(1)} %get-tuple-element.16), channel_id=1, source_target_pairs={{0,2},{1,3},{2,0},{3,1},{4,6},{5,7},{6,4},{7,5},{8,10},{9,11},{10,... | collective-permute-start | bytes 196616 | tf_op jit(solution)/shard_map/ppermute | solution.py:277
  9.3 0.1 collective-permute-start.3
  9.3 0.0 collective-permute-start.4
  9.3 4.3 %collective-permute-start.5 = (bf16[32,1024]{1,0:T(8,128)(2,1)S(1)}, bf16[32,1024]{1,0:T(8,128)(2,1)S(1)}, u32[]{:S(2)}, u32[]{:S(2)}) collective-permute-start(bf16[32,1024]{1,0:T(8,128)(2,1)S(1)} %get-tuple-element.19), channel_id=1, source_target_pairs={{0,8},{1,11},{2,10},{3,9},{4,12},{5,15},{6,14},{7,13},{8,0},{9,3},... | collective-permute-start | bytes 196616 | tf_op jit(solution)/shard_map/ppermute | solution.py:277
  13.6 0.0 collective-permute-done.1.refs_0_
  13.6 0.9 %collective-permute-start.6 = (bf16[32,1024]{1,0:T(8,128)(2,1)S(1)}, bf16[32,1024]{1,0:T(8,128)(2,1)S(1)}, u32[]{:S(2)}, u32[]{:S(2)}) collective-permute-start(bf16[32,1024]{1,0:T(8,128)(2,1)S(1)} %get-tuple-element.20), channel_id=1, source_target_pairs={{0,6},{1,5},{2,4},{3,7},{4,2},{5,1},{6,0},{7,3},{8,14},{9,13},{10,... | collective-permute-start | bytes 196616 | tf_op jit(solution)/shard_map/ppermute | solution.py:277
  14.6 1.5 %collective-permute-start.7 = (bf16[32,1024]{1,0:T(8,128)(2,1)S(1)}, bf16[32,1024]{1,0:T(8,128)(2,1)S(1)}, u32[]{:S(2)}, u32[]{:S(2)}) collective-permute-start(bf16[32,1024]{1,0:T(8,128)(2,1)S(1)} %get-tuple-element.21), channel_id=1, source_target_pairs={{0,10},{1,9},{2,8},{3,11},{4,14},{5,13},{6,12},{7,15},{8,2},{9,1},... | collective-permute-start | bytes 196616 | tf_op jit(solution)/shard_map/ppermute | solution.py:277
  16.1 0.9 %collective-permute-done.3.refs_2_ = bf16[32,1024]{1,0:T(8,128)(2,1)S(1)} collective-permute-done((bf16[32,1024]{1,0:T(8,128)(2,1)S(1)}, bf16[32,1024]{1,0:T(8,128)(2,1)S(1)}, u32[]{:S(2)}, u32[]{:S(2)}) %collective-permute-start.3) | collective-permute-done | bytes 65568 | tf_op jit(solution)/shard_map/ppermute | solution.py:277
  17.1 0.5 %collective-permute-start.8 = (bf16[32,1024]{1,0:T(8,128)(2,1)S(1)}, bf16[32,1024]{1,0:T(8,128)(2,1)S(1)}, u32[]{:S(2)}, u32[]{:S(2)}) collective-permute-start(bf16[32,1024]{1,0:T(8,128)(2,1)S(1)} %collective-permute-done.1.refs_0_), channel_id=1, source_target_pairs={{0,1},{1,0},{2,3},{3,2},{4,5},{5,4},{6,7},{7,6},{8,9},{9,8},{10,11... | collective-permute-start | bytes 196616 | tf_op jit(solution)/shard_map/ppermute | solution.py:281
  17.6 0.1 collective-permute-start.9
  17.6 1.8 %collective-permute-done.6.refs_5_ = bf16[32,1024]{1,0:T(8,128)(2,1)S(1)} collective-permute-done((bf16[32,1024]{1,0:T(8,128)(2,1)S(1)}, bf16[32,1024]{1,0:T(8,128)(2,1)S(1)}, u32[]{:S(2)}, u32[]{:S(2)}) %collective-permute-start.6) | collective-permute-done | bytes 65568 | tf_op jit(solution)/shard_map/ppermute | solution.py:277
  19.5 1.2 %collective-permute-done.7.refs_6_ = bf16[32,1024]{1,0:T(8,128)(2,1)S(1)} collective-permute-done((bf16[32,1024]{1,0:T(8,128)(2,1)S(1)}, bf16[32,1024]{1,0:T(8,128)(2,1)S(1)}, u32[]{:S(2)}, u32[]{:S(2)}) %collective-permute-start.7) | collective-permute-done | bytes 65568 | tf_op jit(solution)/shard_map/ppermute | solution.py:277
  20.7 0.5 %collective-permute-start.12 = (bf16[32,1024]{1,0:T(8,128)(2,1)S(1)}, bf16[32,1024]{1,0:T(8,128)(2,1)S(1)}, u32[]{:S(2)}, u32[]{:S(2)}) collective-permute-start(bf16[32,1024]{1,0:T(8,128)(2,1)S(1)} %collective-permute-done.5.refs_4_), channel_id=1, source_target_pairs={{0,1},{1,0},{2,3},{3,2},{4,5},{5,4},{6,7},{7,6},{8,9},{9,8},{10,11... | collective-permute-start | bytes 196616 | tf_op jit(solution)/shard_map/ppermute | solution.py:281
  21.2 0.1 collective-permute-start.13
  21.3 0.4 %collective-permute-start.14 = (bf16[32,1024]{1,0:T(8,128)(2,1)S(1)}, bf16[32,1024]{1,0:T(8,128)(2,1)S(1)}, u32[]{:S(2)}, u32[]{:S(2)}) collective-permute-start(bf16[32,1024]{1,0:T(8,128)(2,1)S(1)} %collective-permute-done.7.refs_6_), channel_id=1, source_target_pairs={{0,1},{1,0},{2,3},{3,2},{4,5},{5,4},{6,7},{7,6},{8,9},{9,8},{10,11... | collective-permute-start | bytes 196616 | tf_op jit(solution)/shard_map/ppermute | solution.py:281
  21.7 0.2 collective-permute-done.11.refs_10_
  21.9 0.2 collective-permute-done.12.refs_11_
  22.1 0.4 %collective-permute-done.13.refs_12_ = bf16[32,1024]{1,0:T(8,128)(2,1)S(1)} collective-permute-done((bf16[32,1024]{1,0:T(8,128)(2,1)S(1)}, bf16[32,1024]{1,0:T(8,128)(2,1)S(1)}, u32[]{:S(2)}, u32[]{:S(2)}) %collective-permute-start.13) | collective-permute-done | bytes 65568 | tf_op jit(solution)/shard_map/ppermute | solution.py:281
  22.5 0.2 collective-permute-done.14.refs_13_
  22.6 0.6 %score.1 = f32[8,1,128]{2,1,0:T(1,128)S(1)} custom-call(s32[1]{0:T(128)} %bitcast.me_ref, s32[1]{0:T(128)} %bitcast.1.core_ref, bf16[32,1024]{1,0:T(8,128)(2,1)S(1)} %get-tuple-element.14.give_ref, bf16[32,1024]{1,0:T(8,128)(2,1)S(1)} %collective-permute-done.got_ref, bf16[32,1024]{1,0:T(8,128)(2,1)S(1)} %collective-permute-done.1.refs_0_, ...), custom_call_target="tpu_custom_call" | custom-call | tf_op jit(solution)/shard_map/score/pallas_call | solution.py:221
  23.2 10.2 %all_to_all.5.returned_ref = f32[8,1,128]{2,1,0:T(1,128)S(1)} all-to-all(f32[8,1,128]{2,1,0:T(1,128)S(1)} %score.1), channel_id=1, replica_groups=mesh['groups'=2,'docs'=8,'help'=2] {'docs'}, dimensions={0} | all-to-all | bytes 8192 | tf_op jit(solution)/shard_map/all_to_all | solution.py:361
  33.5 0.6 %pick.1 = f32[1,128]{1,0:T(1,128)} custom-call(f32[8,1,128]{2,1,0:T(1,128)S(1)} %all_to_all.5.returned_ref, s32[8,128]{1,0:T(8,128)S(1)} %get-tuple-element.22.place_ref), custom_call_target="tpu_custom_call" | custom-call | tf_op jit(solution)/shard_map/pick/pallas_call | solution.py:261
  (10 shorter events, 0.0 us)
Async XLA Ops:
  2.7 11.0 %collective-permute-start.1 = (bf16[32,1024]{1,0:T(8,128)(2,1)S(1)}, bf16[32,1024]{1,0:T(8,128)(2,1)S(1)}, u32[]{:S(2)}, u32[]{:S(2)}) collective-permute-start(bf16[32,1024]{1,0:T(8,128)(2,1)S(1)} %get-tuple-element.15), channel_id=1, source_target_pairs={{0,12},{1,15},{2,14},{3,13},{4,8},{5,11},{6,10},{7,9},{8,4},{9,7},... | collective-permute-start | bytes 196616 | tf_op jit(solution)/shard_map/ppermute | solution.py:277
  7.8 6.8 %collective-permute-start.2 = (bf16[32,1024]{1,0:T(8,128)(2,1)S(1)}, bf16[32,1024]{1,0:T(8,128)(2,1)S(1)}, u32[]{:S(2)}, u32[]{:S(2)}) collective-permute-start(bf16[32,1024]{1,0:T(8,128)(2,1)S(1)} %get-tuple-element.16), channel_id=1, source_target_pairs={{0,2},{1,3},{2,0},{3,1},{4,6},{5,7},{6,4},{7,5},{8,10},{9,11},{10,... | collective-permute-start | bytes 196616 | tf_op jit(solution)/shard_map/ppermute | solution.py:277
  9.3 7.8 %collective-permute-start.3 = (bf16[32,1024]{1,0:T(8,128)(2,1)S(1)}, bf16[32,1024]{1,0:T(8,128)(2,1)S(1)}, u32[]{:S(2)}, u32[]{:S(2)}) collective-permute-start(bf16[32,1024]{1,0:T(8,128)(2,1)S(1)} %get-tuple-element.17), channel_id=1, source_target_pairs={{0,14},{1,13},{2,12},{3,15},{4,10},{5,9},{6,8},{7,11},{8,6},{9,5},... | collective-permute-start | bytes 196616 | tf_op jit(solution)/shard_map/ppermute | solution.py:277
  9.3 7.7 %collective-permute-start.4 = (bf16[32,1024]{1,0:T(8,128)(2,1)S(1)}, bf16[32,1024]{1,0:T(8,128)(2,1)S(1)}, u32[]{:S(2)}, u32[]{:S(2)}) collective-permute-start(bf16[32,1024]{1,0:T(8,128)(2,1)S(1)} %get-tuple-element.18), channel_id=1, source_target_pairs={{0,4},{1,7},{2,6},{3,5},{4,0},{5,3},{6,2},{7,1},{8,12},{9,15},{10,... | collective-permute-start | bytes 196616 | tf_op jit(solution)/shard_map/ppermute | solution.py:277
  9.3 8.2 %collective-permute-start.5 = (bf16[32,1024]{1,0:T(8,128)(2,1)S(1)}, bf16[32,1024]{1,0:T(8,128)(2,1)S(1)}, u32[]{:S(2)}, u32[]{:S(2)}) collective-permute-start(bf16[32,1024]{1,0:T(8,128)(2,1)S(1)} %get-tuple-element.19), channel_id=1, source_target_pairs={{0,8},{1,11},{2,10},{3,9},{4,12},{5,15},{6,14},{7,13},{8,0},{9,3},... | collective-permute-start | bytes 196616 | tf_op jit(solution)/shard_map/ppermute | solution.py:277
  13.6 5.8 %collective-permute-start.6 = (bf16[32,1024]{1,0:T(8,128)(2,1)S(1)}, bf16[32,1024]{1,0:T(8,128)(2,1)S(1)}, u32[]{:S(2)}, u32[]{:S(2)}) collective-permute-start(bf16[32,1024]{1,0:T(8,128)(2,1)S(1)} %get-tuple-element.20), channel_id=1, source_target_pairs={{0,6},{1,5},{2,4},{3,7},{4,2},{5,1},{6,0},{7,3},{8,14},{9,13},{10,... | collective-permute-start | bytes 196616 | tf_op jit(solution)/shard_map/ppermute | solution.py:277
  14.6 6.1 %collective-permute-start.7 = (bf16[32,1024]{1,0:T(8,128)(2,1)S(1)}, bf16[32,1024]{1,0:T(8,128)(2,1)S(1)}, u32[]{:S(2)}, u32[]{:S(2)}) collective-permute-start(bf16[32,1024]{1,0:T(8,128)(2,1)S(1)} %get-tuple-element.21), channel_id=1, source_target_pairs={{0,10},{1,9},{2,8},{3,11},{4,14},{5,13},{6,12},{7,15},{8,2},{9,1},... | collective-permute-start | bytes 196616 | tf_op jit(solution)/shard_map/ppermute | solution.py:277
  17.0 3.6 %collective-permute-start = (bf16[32,1024]{1,0:T(8,128)(2,1)S(1)}, bf16[32,1024]{1,0:T(8,128)(2,1)S(1)}, u32[]{:S(2)}, u32[]{:S(2)}) collective-permute-start(bf16[32,1024]{1,0:T(8,128)(2,1)S(1)} %get-tuple-element.14.give_ref), channel_id=1, source_target_pairs={{0,1},{1,0},{2,3},{3,2},{4,5},{5,4},{6,7},{7,6},{8,9},{9,8},{10,11... | collective-permute-start | bytes 196616 | tf_op jit(solution)/shard_map/ppermute | solution.py:281
  17.1 4.1 %collective-permute-start.8 = (bf16[32,1024]{1,0:T(8,128)(2,1)S(1)}, bf16[32,1024]{1,0:T(8,128)(2,1)S(1)}, u32[]{:S(2)}, u32[]{:S(2)}) collective-permute-start(bf16[32,1024]{1,0:T(8,128)(2,1)S(1)} %collective-permute-done.1.refs_0_), channel_id=1, source_target_pairs={{0,1},{1,0},{2,3},{3,2},{4,5},{5,4},{6,7},{7,6},{8,9},{9,8},{10,11... | collective-permute-start | bytes 196616 | tf_op jit(solution)/shard_map/ppermute | solution.py:281
  17.6 3.7 %collective-permute-start.9 = (bf16[32,1024]{1,0:T(8,128)(2,1)S(1)}, bf16[32,1024]{1,0:T(8,128)(2,1)S(1)}, u32[]{:S(2)}, u32[]{:S(2)}) collective-permute-start(bf16[32,1024]{1,0:T(8,128)(2,1)S(1)} %collective-permute-done.2.refs_1_), channel_id=1, source_target_pairs={{0,1},{1,0},{2,3},{3,2},{4,5},{5,4},{6,7},{7,6},{8,9},{9,8},{10,11... | collective-permute-start | bytes 196616 | tf_op jit(solution)/shard_map/ppermute | solution.py:281
  19.5 2.3 %collective-permute-start.10 = (bf16[32,1024]{1,0:T(8,128)(2,1)S(1)}, bf16[32,1024]{1,0:T(8,128)(2,1)S(1)}, u32[]{:S(2)}, u32[]{:S(2)}) collective-permute-start(bf16[32,1024]{1,0:T(8,128)(2,1)S(1)} %collective-permute-done.3.refs_2_), channel_id=1, source_target_pairs={{0,1},{1,0},{2,3},{3,2},{4,5},{5,4},{6,7},{7,6},{8,9},{9,8},{10,11... | collective-permute-start | bytes 196616 | tf_op jit(solution)/shard_map/ppermute | solution.py:281
  20.7 1.3 %collective-permute-start.11 = (bf16[32,1024]{1,0:T(8,128)(2,1)S(1)}, bf16[32,1024]{1,0:T(8,128)(2,1)S(1)}, u32[]{:S(2)}, u32[]{:S(2)}) collective-permute-start(bf16[32,1024]{1,0:T(8,128)(2,1)S(1)} %collective-permute-done.4.refs_3_), channel_id=1, source_target_pairs={{0,1},{1,0},{2,3},{3,2},{4,5},{5,4},{6,7},{7,6},{8,9},{9,8},{10,11... | collective-permute-start | bytes 196616 | tf_op jit(solution)/shard_map/ppermute | solution.py:281
  20.7 1.4 %collective-permute-start.12 = (bf16[32,1024]{1,0:T(8,128)(2,1)S(1)}, bf16[32,1024]{1,0:T(8,128)(2,1)S(1)}, u32[]{:S(2)}, u32[]{:S(2)}) collective-permute-start(bf16[32,1024]{1,0:T(8,128)(2,1)S(1)} %collective-permute-done.5.refs_4_), channel_id=1, source_target_pairs={{0,1},{1,0},{2,3},{3,2},{4,5},{5,4},{6,7},{7,6},{8,9},{9,8},{10,11... | collective-permute-start | bytes 196616 | tf_op jit(solution)/shard_map/ppermute | solution.py:281
  21.2 1.3 %collective-permute-start.13 = (bf16[32,1024]{1,0:T(8,128)(2,1)S(1)}, bf16[32,1024]{1,0:T(8,128)(2,1)S(1)}, u32[]{:S(2)}, u32[]{:S(2)}) collective-permute-start(bf16[32,1024]{1,0:T(8,128)(2,1)S(1)} %collective-permute-done.6.refs_5_), channel_id=1, source_target_pairs={{0,1},{1,0},{2,3},{3,2},{4,5},{5,4},{6,7},{7,6},{8,9},{9,8},{10,11... | collective-permute-start | bytes 196616 | tf_op jit(solution)/shard_map/ppermute | solution.py:281
  21.3 1.3 %collective-permute-start.14 = (bf16[32,1024]{1,0:T(8,128)(2,1)S(1)}, bf16[32,1024]{1,0:T(8,128)(2,1)S(1)}, u32[]{:S(2)}, u32[]{:S(2)}) collective-permute-start(bf16[32,1024]{1,0:T(8,128)(2,1)S(1)} %collective-permute-done.7.refs_6_), channel_id=1, source_target_pairs={{0,1},{1,0},{2,3},{3,2},{4,5},{5,4},{6,7},{7,6},{8,9},{9,8},{10,11... | collective-permute-start | bytes 196616 | tf_op jit(solution)/shard_map/ppermute | solution.py:281

commit v3 on v1

v3 whole, which is shorter than its diff:
```python
import functools

import jax
import jax.numpy as jnp
from jax import lax
from jax.experimental import pallas as pl
from jax.experimental.pallas import tpu as pltpu
from jax.sharding import PartitionSpec as P

CL_OWN = 1
LANES = 128
EMPTY = 2.0
VMEM = pl.BlockSpec(memory_space=pltpu.VMEM)
SMEM = pl.BlockSpec(memory_space=pltpu.SMEM)
HBM = pl.BlockSpec(memory_space=pltpu.HBM)
PARAMS = pltpu.CompilerParams(vmem_limit_bytes=32 * 2**20)

ORDER = ((6, 1, 7, 2, 4, 3, 5), (6, 1, 7, 2, 4, 3, 5))


def iota(shape, dim):
    return lax.broadcasted_iota(jnp.int32, shape, dim)


def in_hbm(array):
    return pltpu.with_memory_space_constraint(array, pltpu.HBM)


def in_vmem(array):
    return pltpu.with_memory_space_constraint(array, pltpu.VMEM)


def embed_kernel(
    slot_cap, block_of, me_ref, core_ref,
    tok_hbm, len_hbm, id_hbm, weight_hbm, bias_hbm, *refs,
):
    *packed_refs, place_ref, tok, weight, bias, lens, ids, sems = refs
    rows, seq_len, _ = tok.shape
    slots = sum(ref.shape[0] for ref in packed_refs)
    pairs = ((len_hbm, lens), (id_hbm, ids), (tok_hbm, tok), (weight_hbm, weight), (bias_hbm, bias))
    copies = [
        pltpu.make_async_copy(source, target, sems.at[at])
        for at, (source, target) in enumerate(pairs)
    ]
    for copy in copies:
        copy.start()
    diagonal = iota((rows, rows), 0) == iota((rows, rows), 1)

    def column(row):
        return jnp.sum(jnp.where(diagonal, row, 0), axis=1, keepdims=True)

    copies[0].wait()
    copies[1].wait()
    counts = column(lens[...])
    owner = ids[...] // CL_OWN
    earlier = (column(owner) == owner) & (iota((rows, rows), 0) < iota((rows, rows), 1))
    rank = jnp.sum(earlier.astype(jnp.int32), axis=0, keepdims=True)
    place_ref[0:1, :] = owner
    place_ref[1:2, :] = rank
    block = block_of(owner, me_ref, core_ref)
    chooser = iota((slots, rows), 0) == block * slot_cap + rank
    chooser = jnp.where(chooser, 1.0, 0.0)
    empty = jnp.sum(chooser, axis=1, keepdims=True) < 0.5
    copies[2].wait()
    summed = tok[:, 0, :].astype(jnp.float32)
    for t in range(1, seq_len):
        summed += jnp.where(counts > t, tok[:, t, :].astype(jnp.float32), 0.0)
    pooled = (summed / counts.astype(jnp.float32)).astype(jnp.bfloat16)
    copies[3].wait()
    copies[4].wait()
    hidden = jnp.tanh(
        jnp.dot(pooled, weight[...], preferred_element_type=jnp.float32) + bias[...]
    )
    factor = lax.rsqrt(jnp.sum(hidden * hidden, axis=1, keepdims=True) + 1e-06)
    embedded = (hidden * factor).astype(jnp.bfloat16)
    packed = jnp.dot(chooser.astype(jnp.bfloat16), embedded, preferred_element_type=jnp.float32)
    first = packed[:, 0:LANES]
    first = jnp.where(empty & (iota(first.shape, 1) == 0), EMPTY, first).astype(jnp.bfloat16)
    rest = packed[:, LANES:].astype(jnp.bfloat16)
    at = 0
    for ref in packed_refs:
        ref[:, 0:LANES] = first[at : at + ref.shape[0]]
        ref[:, LANES:] = rest[at : at + ref.shape[0]]
        at += ref.shape[0]


def order_block(owner, me_ref, core_ref):
    step = owner ^ me_ref[0]
    block = jnp.zeros_like(step)
    for at, steps in enumerate(zip(*ORDER), 1):
        block = jnp.where(step == jnp.where(core_ref[0] == 0, *steps), at, block)
    return block


def owner_block(owner, *_):
    return owner


def embed(me, core, arrays, sizes, slot_cap, block_of):
    token_states, lengths, cluster_id, proj_weight, proj_bias = arrays
    rows, _, width = token_states.shape
    return pl.pallas_call(
        functools.partial(embed_kernel, slot_cap, block_of),
        out_shape=[jax.ShapeDtypeStruct((size, width), jnp.bfloat16) for size in sizes]
        + [jax.ShapeDtypeStruct((8, rows), jnp.int32)],
        in_specs=[SMEM] * 2 + [HBM] * 5,
        out_specs=[VMEM] * (len(sizes) + 1),
        scratch_shapes=[
            pltpu.VMEM(token_states.shape, token_states.dtype),
            pltpu.VMEM(proj_weight.shape, proj_weight.dtype),
            pltpu.VMEM((1, width), jnp.float32),
            pltpu.VMEM((1, rows), jnp.int32),
            pltpu.VMEM((1, rows), jnp.int32),
            pltpu.SemaphoreType.DMA((5,)),
        ],
        compiler_params=PARAMS,
        name="embed",
    )(
        me,
        core,
        in_hbm(token_states),
        in_hbm(lengths.reshape(1, rows)),
        in_hbm(cluster_id.reshape(1, rows)),
        in_hbm(proj_weight),
        in_hbm(proj_bias.reshape(1, width)),
    )


def join_kernel(*refs):
    *in_refs, out_ref = refs
    at = 0
    for ref in in_refs:
        out_ref[pl.ds(at, ref.shape[0]), :] = ref[...]
        at += ref.shape[0]


def join(blocks):
    rows = sum(block.shape[0] for block in blocks)
    return pl.pallas_call(
        join_kernel,
        out_shape=jax.ShapeDtypeStruct((rows, blocks[0].shape[1]), blocks[0].dtype),
        in_specs=[VMEM] * len(blocks),
        out_specs=VMEM,
        compiler_params=PARAMS,
        name="join",
    )(*blocks)


def best_of(ref, columns, same):
    scores = lax.dot_general(
        ref[...], columns, (((1,), (1,)), ((), ())), preferred_element_type=jnp.float32
    )
    valid = ref[:, 0:LANES].astype(jnp.float32)[:, 0:1] < 1.5
    if same:
        valid = valid & (iota(scores.shape, 0) != iota(scores.shape, 1))
    return jnp.max(jnp.where(valid, scores, -1.0), axis=0, keepdims=True)


def score_kernel(slot_cap, sources_of, me_ref, core_ref, mine_ref, other_ref, out_ref):
    columns = mine_ref[...]
    maxima = jnp.maximum(best_of(mine_ref, columns, True), best_of(other_ref, columns, False))
    for at, source in enumerate(sources_of(out_ref.shape[0], me_ref, core_ref)):
        out_ref[source, :, 0:slot_cap] = maxima[:, at * slot_cap : (at + 1) * slot_cap]


def order_sources(owners, me_ref, core_ref):
    steps = [jnp.where(core_ref[0] == 0, *steps) for steps in zip(*ORDER)]
    return [me_ref[0]] + [me_ref[0] ^ step for step in steps]


def owner_sources(owners, *_):
    return range(owners)


def score(me, core, mine, other, owners, slot_cap, sources_of):
    lanes = -(-slot_cap // LANES) * LANES
    return pl.pallas_call(
        functools.partial(score_kernel, slot_cap, sources_of),
        out_shape=jax.ShapeDtypeStruct((owners, 1, lanes), jnp.float32),
        in_specs=[SMEM] * 2 + [VMEM] * 2,
        out_specs=VMEM,
        compiler_params=PARAMS,
        name="score",
    )(me, core, mine, other)


def pick_kernel(returned_ref, place_ref, out_ref):
    owners, _, lanes = returned_ref.shape
    rows = place_ref.shape[1]
    owner = place_ref[0:1, :]
    rank = jnp.broadcast_to(place_ref[1:2, :], (owners, rows))
    returned = returned_ref[...].reshape(owners, lanes)
    taken = jnp.take_along_axis(returned, rank, axis=1, mode="promise_in_bounds")
    taken = jnp.where(iota((owners, rows), 0) == owner, taken, -3.0)
    out_ref[...] = jnp.max(taken, axis=0, keepdims=True)


def pick(returned, place):
    rows = place.shape[1]
    return pl.pallas_call(
        pick_kernel,
        out_shape=jax.ShapeDtypeStruct((1, rows), jnp.float32),
        in_specs=[VMEM, VMEM],
        out_specs=VMEM,
        name="pick",
    )(in_vmem(returned), in_vmem(place)).reshape(rows)


def step_to(value, steps):
    helpers = lax.axis_size("help")
    pairs = [
        (doc * helpers + core, (doc ^ steps[core]) * helpers + core)
        for doc in range(lax.axis_size("docs"))
        for core in range(helpers)
    ]
    return lax.ppermute(value, ("docs", "help"), pairs)


def swap(value):
    return lax.ppermute(value, "help", [(i, i ^ 1) for i in range(lax.axis_size("help"))])


def body(*arrays):
    owners = lax.axis_size("docs")
    slot_cap = 2 * arrays[0].shape[0] // owners
    me = lax.axis_index("docs").reshape(1)
    core = lax.axis_index("help").reshape(1)
    if owners == len(ORDER[0]) + 1:
        block_of, sources_of = order_block, order_sources
        own, *blocks, place = embed(me, core, arrays, [slot_cap] * owners, slot_cap, block_of)
        mine = join([own] + [step_to(*send) for send in zip(blocks, zip(*ORDER))])
    else:
        block_of, sources_of = owner_block, owner_sources
        packed, place = embed(me, core, arrays, [owners * slot_cap], slot_cap, block_of)
        mine = lax.all_to_all(packed, "docs", split_axis=0, concat_axis=0, tiled=True)
    maxima = score(me, core, mine, swap(mine), owners, slot_cap, sources_of)
    returned = lax.all_to_all(maxima, "docs", split_axis=0, concat_axis=0, tiled=True)
    return pick(returned, place)


def solution(mesh):
    spread = P(("groups", "docs", "help"))
    in_specs = (P(("groups", "docs", "help"), None, None), spread, spread, P(), P())
    return jax.shard_map(body, mesh=mesh, in_specs=in_specs, out_specs=spread, check_vma=False)
```

time: 38.2 us -> 33.5 us (0.88)
  blocking collectives: 31.5 us -> 9.51 us
  starting transfers between devices: 0.01 us -> 13.3 us
  waiting for transfers between devices: 1.9 us -> 6.7 us
  Pallas kernels: 4.51 us -> 3.84 us
    all_to_all x1 -> x0, blocking collectives: 21.6 us -> none  [body(): lax.all_to_all(packed, 'docs', split_axis=0, concat_axis=0, tiled=True)]
    ppermute x1 -> x8, starting transfers between devices: 0.01 us -> 13.3 us  [the longest x7 13.2 us: step_to(): return lax.ppermute(value, ('docs', 'help'), pairs)]
    ppermute x1 -> x8, waiting for transfers between devices: 1.9 us -> 6.7 us  [the longest x7 4.81 us: step_to(): return lax.ppermute(value, ('docs', 'help'), pairs)]
    pallas_call x1, Pallas kernels: 1.27 us -> 0.59 us  [pick(): pl.pallas_call(pick_kernel, out_shape=jax.ShapeDtypeStruct((1, rows), jnp...]
    all_to_all x1, blocking collectives: 9.95 us -> 9.51 us  [body(): lax.all_to_all(maxima, 'docs', split_axis=0, concat_axis=0, tiled=True)]
    pallas_call x2 -> x3, Pallas kernels: 3.23 us -> 3.24 us  [the longest x1 2.66 us: embed(): pl.pallas_call(functools.partial(embed_kernel, slot_cap, block_of), out_s...]
  transfers between devices with their start and end apart: 1 -> 8, of which waited for: 1 -> 4; matrix products, arithmetic and copies ran while one was open for 0% -> 0% of each run, Pallas kernels for 0% -> 0%
where the time goes in v3:
time: 33.5 us; the launch traced here: 33.3 us
  starting transfers between devices  13.3 us (40%)
  blocking collectives  9.51 us (28%)
  waiting for transfers between devices  6.7 us (20%)
  Pallas kernels  3.84 us (11%)
    ppermute x7, starting transfers between devices, step_to(): return lax.ppermute(value, ('docs', 'help'), pairs)  13.2 us
    all_to_all x1, blocking collectives, body(): lax.all_to_all(maxima, 'docs', split_axis=0, concat_axis=0, tiled=True)  9.51 us
    ppermute x7, waiting for transfers between devices, step_to(): return lax.ppermute(value, ('docs', 'help'), pairs)  4.81 us
    pallas_call x1, Pallas kernels, embed(): pl.pallas_call(functools.partial(embed_kernel, slot_cap, block_of), out_s...  2.66 us
    ppermute x1, waiting for transfers between devices, swap(): lax.ppermute(value, 'help', [(i, i ^ 1) for i in range(lax.axis_size('hel...  1.9 us
  transfers between devices with their start and end apart: 8, of which 4 were waited for; matrix products, arithmetic and copies ran while one was open for 0% of the time, Pallas kernels for 0%

profile of v3, /device:TPU:0, one launch (start us, length us, event | category | flops | bytes accessed | tf_op | source)
XLA Modules:
  0.0 33.3 jit_solution(17540438096783005746)
XLA Ops:
  0.0 2.7 %embed.1 = (bf16[32,1024]{1,0:T(8,128)(2,1)S(1)}, bf16[32,1024]{1,0:T(8,128)(2,1)S(1)}, bf16[32,1024]{1,0:T(8,128)(2,1)S(1)}, bf16[32,1024]{1,0:T(8,128)(2,1)S(1...) custom-call(s32[1]{0:T(128)} %bitcast.me_ref, ...), custom_call_target="tpu_custom_call" | custom-call | tf_op jit(solution)/shard_map/embed/pallas_call | solution.py:102
  2.7 5.1 %collective-permute-start = (bf16[32,1024]{1,0:T(8,128)(2,1)S(1)}, bf16[32,1024]{1,0:T(8,128)(2,1)S(1)}, u32[]{:S(2)}, u32[]{:S(2)}) collective-permute-start(bf16[32,1024]{1,0:T(8,128)(2,1)S(1)} %get-tuple-element.15), channel_id=1, source_target_pairs={{0,12},{1,13},{2,14},{3,15},{4,8},{5,9},{6,10},{7,11},{8,4},{9,5},... | collective-permute-start | bytes 196616 | tf_op jit(solution)/shard_map/ppermute | solution.py:216
  7.8 1.5 %collective-permute-start.1 = (bf16[32,1024]{1,0:T(8,128)(2,1)S(1)}, bf16[32,1024]{1,0:T(8,128)(2,1)S(1)}, u32[]{:S(2)}, u32[]{:S(2)}) collective-permute-start(bf16[32,1024]{1,0:T(8,128)(2,1)S(1)} %get-tuple-element.16), channel_id=1, source_target_pairs={{0,2},{1,3},{2,0},{3,1},{4,6},{5,7},{6,4},{7,5},{8,10},{9,11},{10,... | collective-permute-start | bytes 196616 | tf_op jit(solution)/shard_map/ppermute | solution.py:216
  9.3 0.1 collective-permute-start.2
  9.3 0.0 collective-permute-start.3
  9.3 4.3 %collective-permute-start.4 = (bf16[32,1024]{1,0:T(8,128)(2,1)S(1)}, bf16[32,1024]{1,0:T(8,128)(2,1)S(1)}, u32[]{:S(2)}, u32[]{:S(2)}) collective-permute-start(bf16[32,1024]{1,0:T(8,128)(2,1)S(1)} %get-tuple-element.19), channel_id=1, source_target_pairs={{0,8},{1,9},{2,10},{3,11},{4,12},{5,13},{6,14},{7,15},{8,0},{9,1},... | collective-permute-start | bytes 196616 | tf_op jit(solution)/shard_map/ppermute | solution.py:216
  13.6 0.0 collective-permute-done.refs_1_
  13.6 0.9 %collective-permute-start.5 = (bf16[32,1024]{1,0:T(8,128)(2,1)S(1)}, bf16[32,1024]{1,0:T(8,128)(2,1)S(1)}, u32[]{:S(2)}, u32[]{:S(2)}) collective-permute-start(bf16[32,1024]{1,0:T(8,128)(2,1)S(1)} %get-tuple-element.20), channel_id=1, source_target_pairs={{0,6},{1,7},{2,4},{3,5},{4,2},{5,3},{6,0},{7,1},{8,14},{9,15},{10,... | collective-permute-start | bytes 196616 | tf_op jit(solution)/shard_map/ppermute | solution.py:216
  14.6 0.0 collective-permute-done.1.refs_2_
  14.6 1.3 %collective-permute-start.6 = (bf16[32,1024]{1,0:T(8,128)(2,1)S(1)}, bf16[32,1024]{1,0:T(8,128)(2,1)S(1)}, u32[]{:S(2)}, u32[]{:S(2)}) collective-permute-start(bf16[32,1024]{1,0:T(8,128)(2,1)S(1)} %get-tuple-element.21), channel_id=1, source_target_pairs={{0,10},{1,11},{2,8},{3,9},{4,14},{5,15},{6,12},{7,13},{8,2},{9,3},... | collective-permute-start | bytes 196616 | tf_op jit(solution)/shard_map/ppermute | solution.py:216
  15.9 1.1 %collective-permute-done.2.refs_3_ = bf16[32,1024]{1,0:T(8,128)(2,1)S(1)} collective-permute-done((bf16[32,1024]{1,0:T(8,128)(2,1)S(1)}, bf16[32,1024]{1,0:T(8,128)(2,1)S(1)}, u32[]{:S(2)}, u32[]{:S(2)}) %collective-permute-start.2) | collective-permute-done | bytes 65568 | tf_op jit(solution)/shard_map/ppermute | solution.py:216
  17.0 0.0 collective-permute-done.3.refs_4_
  17.0 0.0 collective-permute-done.4.refs_5_
  17.0 2.5 %collective-permute-done.5.refs_6_ = bf16[32,1024]{1,0:T(8,128)(2,1)S(1)} collective-permute-done((bf16[32,1024]{1,0:T(8,128)(2,1)S(1)}, bf16[32,1024]{1,0:T(8,128)(2,1)S(1)}, u32[]{:S(2)}, u32[]{:S(2)}) %collective-permute-start.5) | collective-permute-done | bytes 65568 | tf_op jit(solution)/shard_map/ppermute | solution.py:216
  19.5 1.2 %collective-permute-done.6.refs_7_ = bf16[32,1024]{1,0:T(8,128)(2,1)S(1)} collective-permute-done((bf16[32,1024]{1,0:T(8,128)(2,1)S(1)}, bf16[32,1024]{1,0:T(8,128)(2,1)S(1)}, u32[]{:S(2)}, u32[]{:S(2)}) %collective-permute-start.6) | collective-permute-done | bytes 65568 | tf_op jit(solution)/shard_map/ppermute | solution.py:216
  20.7 0.1 collective-permute-start.7
  20.8 1.9 %collective-permute-done.7.other_ref = bf16[256,1024]{1,0:T(8,128)(2,1)S(1)} collective-permute-done((bf16[256,1024]{1,0:T(8,128)(2,1)S(1)}, bf16[256,1024]{1,0:T(8,128)(2,1)S(1)}, u32[]{:S(2)}, u32[]{:S(2)}) %collective-permute-start.7) | collective-permute-done | bytes 524320 | tf_op jit(solution)/shard_map/ppermute | solution.py:220
  22.7 0.5 %score.1 = f32[8,1,128]{2,1,0:T(1,128)S(1)} custom-call(s32[1]{0:T(128)} %bitcast.me_ref, s32[1]{0:T(128)} %bitcast.1.core_ref, bf16[256,1024]{1,0:T(8,128)(2,1)S(1)} %join.1.mine_ref, bf16[256,1024]{1,0:T(8,128)(2,1)S(1)} %collective-permute-done.7.other_ref), custom_call_target="tpu_custom_call" | custom-call | tf_op jit(solution)/shard_map/score/pallas_call | solution.py:177
  23.2 9.5 %all_to_all.5.returned_ref = f32[8,1,128]{2,1,0:T(1,128)S(1)} all-to-all(f32[8,1,128]{2,1,0:T(1,128)S(1)} %score.1), channel_id=1, replica_groups=mesh['groups'=2,'docs'=8,'help'=2] {'docs'}, dimensions={0} | all-to-all | bytes 8192 | tf_op jit(solution)/shard_map/all_to_all | solution.py:237
  32.8 0.6 %pick.1 = f32[1,128]{1,0:T(1,128)} custom-call(f32[8,1,128]{2,1,0:T(1,128)S(1)} %all_to_all.5.returned_ref, s32[8,128]{1,0:T(8,128)S(1)} %get-tuple-element.22.place_ref), custom_call_target="tpu_custom_call" | custom-call | tf_op jit(solution)/shard_map/pick/pallas_call | solution.py:200
  (1 shorter events, 0.0 us)
Async XLA Ops:
  2.7 11.0 %collective-permute-start = (bf16[32,1024]{1,0:T(8,128)(2,1)S(1)}, bf16[32,1024]{1,0:T(8,128)(2,1)S(1)}, u32[]{:S(2)}, u32[]{:S(2)}) collective-permute-start(bf16[32,1024]{1,0:T(8,128)(2,1)S(1)} %get-tuple-element.15), channel_id=1, source_target_pairs={{0,12},{1,13},{2,14},{3,15},{4,8},{5,9},{6,10},{7,11},{8,4},{9,5},... | collective-permute-start | bytes 196616 | tf_op jit(solution)/shard_map/ppermute | solution.py:216
  7.8 6.8 %collective-permute-start.1 = (bf16[32,1024]{1,0:T(8,128)(2,1)S(1)}, bf16[32,1024]{1,0:T(8,128)(2,1)S(1)}, u32[]{:S(2)}, u32[]{:S(2)}) collective-permute-start(bf16[32,1024]{1,0:T(8,128)(2,1)S(1)} %get-tuple-element.16), channel_id=1, source_target_pairs={{0,2},{1,3},{2,0},{3,1},{4,6},{5,7},{6,4},{7,5},{8,10},{9,11},{10,... | collective-permute-start | bytes 196616 | tf_op jit(solution)/shard_map/ppermute | solution.py:216
  9.3 7.7 %collective-permute-start.2 = (bf16[32,1024]{1,0:T(8,128)(2,1)S(1)}, bf16[32,1024]{1,0:T(8,128)(2,1)S(1)}, u32[]{:S(2)}, u32[]{:S(2)}) collective-permute-start(bf16[32,1024]{1,0:T(8,128)(2,1)S(1)} %get-tuple-element.17), channel_id=1, source_target_pairs={{0,14},{1,15},{2,12},{3,13},{4,10},{5,11},{6,8},{7,9},{8,6},{9,7},... | collective-permute-start | bytes 196616 | tf_op jit(solution)/shard_map/ppermute | solution.py:216
  9.3 7.7 %collective-permute-start.3 = (bf16[32,1024]{1,0:T(8,128)(2,1)S(1)}, bf16[32,1024]{1,0:T(8,128)(2,1)S(1)}, u32[]{:S(2)}, u32[]{:S(2)}) collective-permute-start(bf16[32,1024]{1,0:T(8,128)(2,1)S(1)} %get-tuple-element.18), channel_id=1, source_target_pairs={{0,4},{1,5},{2,6},{3,7},{4,0},{5,1},{6,2},{7,3},{8,12},{9,13},{10,... | collective-permute-start | bytes 196616 | tf_op jit(solution)/shard_map/ppermute | solution.py:216
  9.3 7.7 %collective-permute-start.4 = (bf16[32,1024]{1,0:T(8,128)(2,1)S(1)}, bf16[32,1024]{1,0:T(8,128)(2,1)S(1)}, u32[]{:S(2)}, u32[]{:S(2)}) collective-permute-start(bf16[32,1024]{1,0:T(8,128)(2,1)S(1)} %get-tuple-element.19), channel_id=1, source_target_pairs={{0,8},{1,9},{2,10},{3,11},{4,12},{5,13},{6,14},{7,15},{8,0},{9,1},... | collective-permute-start | bytes 196616 | tf_op jit(solution)/shard_map/ppermute | solution.py:216
  13.6 5.8 %collective-permute-start.5 = (bf16[32,1024]{1,0:T(8,128)(2,1)S(1)}, bf16[32,1024]{1,0:T(8,128)(2,1)S(1)}, u32[]{:S(2)}, u32[]{:S(2)}) collective-permute-start(bf16[32,1024]{1,0:T(8,128)(2,1)S(1)} %get-tuple-element.20), channel_id=1, source_target_pairs={{0,6},{1,7},{2,4},{3,5},{4,2},{5,3},{6,0},{7,1},{8,14},{9,15},{10,... | collective-permute-start | bytes 196616 | tf_op jit(solution)/shard_map/ppermute | solution.py:216
  14.6 6.1 %collective-permute-start.6 = (bf16[32,1024]{1,0:T(8,128)(2,1)S(1)}, bf16[32,1024]{1,0:T(8,128)(2,1)S(1)}, u32[]{:S(2)}, u32[]{:S(2)}) collective-permute-start(bf16[32,1024]{1,0:T(8,128)(2,1)S(1)} %get-tuple-element.21), channel_id=1, source_target_pairs={{0,10},{1,11},{2,8},{3,9},{4,14},{5,15},{6,12},{7,13},{8,2},{9,3},... | collective-permute-start | bytes 196616 | tf_op jit(solution)/shard_map/ppermute | solution.py:216
  20.7 2.0 %collective-permute-start.7 = (bf16[256,1024]{1,0:T(8,128)(2,1)S(1)}, bf16[256,1024]{1,0:T(8,128)(2,1)S(1)}, u32[]{:S(2)}, u32[]{:S(2)}) collective-permute-start(bf16[256,1024]{1,0:T(8,128)(2,1)S(1)} %join.1.mine_ref), channel_id=1, source_target_pairs={{0,1},{1,0},{2,3},{3,2},{4,5},{5,4},{6,7},{7,6},{8,9},{9,8},{10,11... | collective-permute-start | bytes 1572872 | tf_op jit(solution)/shard_map/ppermute | solution.py:220

commit v4 on v3

--- a/solution.py
+++ b/solution.py
@@ -10,6 +10,7 @@
 CL_OWN = 1
 LANES = 128
 EMPTY = 2.0
+WEIGHT_PARTS = 8
 VMEM = pl.BlockSpec(memory_space=pltpu.VMEM)
 SMEM = pl.BlockSpec(memory_space=pltpu.SMEM)
 HBM = pl.BlockSpec(memory_space=pltpu.HBM)
@@ -18,6 +19,14 @@
 ORDER = ((6, 1, 7, 2, 4, 3, 5), (6, 1, 7, 2, 4, 3, 5))
 
 
+def turn(doc):
+    return (doc >> 2) & 1
+
+
+def kind(doc):
+    return ((doc >> 1) ^ (doc >> 2)) & 1
+
+
 def iota(shape, dim):
     return lax.broadcasted_iota(jnp.int32, shape, dim)
 
@@ -31,13 +40,16 @@
 
 
 def embed_kernel(
-    slot_cap, block_of, me_ref, core_ref,
+    slot_cap, block_of, me_ref,
     tok_hbm, len_hbm, id_hbm, weight_hbm, bias_hbm, *refs,
 ):
     *packed_refs, place_ref, tok, weight, bias, lens, ids, sems = refs
     rows, seq_len, _ = tok.shape
     slots = sum(ref.shape[0] for ref in packed_refs)
-    pairs = ((len_hbm, lens), (id_hbm, ids), (tok_hbm, tok), (weight_hbm, weight), (bias_hbm, bias))
+    pairs = [(len_hbm, lens), (id_hbm, ids), (tok_hbm, tok), (bias_hbm, bias)]
+    part = weight.shape[0] // WEIGHT_PARTS
+    for at in range(WEIGHT_PARTS):
+        pairs.append((weight_hbm.at[pl.ds(at * part, part)], weight.at[pl.ds(at * part, part)]))
     copies = [
         pltpu.make_async_copy(source, target, sems.at[at])
         for at, (source, target) in enumerate(pairs)
@@ -57,7 +69,7 @@
     rank = jnp.sum(earlier.astype(jnp.int32), axis=0, keepdims=True)
     place_ref[0:1, :] = owner
     place_ref[1:2, :] = rank
-    block = block_of(owner, me_ref, core_ref)
+    block = block_of(owner, me_ref[0])
     chooser = iota((slots, rows), 0) == block * slot_cap + rank
     chooser = jnp.where(chooser, 1.0, 0.0)
     empty = jnp.sum(chooser, axis=1, keepdims=True) < 0.5
@@ -66,8 +78,8 @@
     for t in range(1, seq_len):
         summed += jnp.where(counts > t, tok[:, t, :].astype(jnp.float32), 0.0)
     pooled = (summed / counts.astype(jnp.float32)).astype(jnp.bfloat16)
-    copies[3].wait()
-    copies[4].wait()
+    for copy in copies[3:]:
+        copy.wait()
     hidden = jnp.tanh(
         jnp.dot(pooled, weight[...], preferred_element_type=jnp.float32) + bias[...]
     )
@@ -84,26 +96,26 @@
         at += ref.shape[0]
 
 
-def order_block(owner, me_ref, core_ref):
-    step = owner ^ me_ref[0]
+def order_block(owner, me):
+    step = owner ^ me
     block = jnp.zeros_like(step)
     for at, steps in enumerate(zip(*ORDER), 1):
-        block = jnp.where(step == jnp.where(core_ref[0] == 0, *steps), at, block)
+        block = jnp.where(step == jnp.where(kind(me) == 0, *steps), at, block)
     return block
 
 
-def owner_block(owner, *_):
+def owner_block(owner, _):
     return owner
 
 
-def embed(me, core, arrays, sizes, slot_cap, block_of):
+def embed(me, arrays, sizes, slot_cap, block_of):
     token_states, lengths, cluster_id, proj_weight, proj_bias = arrays
     rows, _, width = token_states.shape
     return pl.pallas_call(
         functools.partial(embed_kernel, slot_cap, block_of),
         out_shape=[jax.ShapeDtypeStruct((size, width), jnp.bfloat16) for size in sizes]
         + [jax.ShapeDtypeStruct((8, rows), jnp.int32)],
-        in_specs=[SMEM] * 2 + [HBM] * 5,
+        in_specs=[SMEM] + [HBM] * 5,
         out_specs=[VMEM] * (len(sizes) + 1),
         scratch_shapes=[
             pltpu.VMEM(token_states.shape, token_states.dtype),
@@ -111,13 +123,12 @@
             pltpu.VMEM((1, width), jnp.float32),
             pltpu.VMEM((1, rows), jnp.int32),
             pltpu.VMEM((1, rows), jnp.int32),
-            pltpu.SemaphoreType.DMA((5,)),
+            pltpu.SemaphoreType.DMA((4 + WEIGHT_PARTS,)),
         ],
         compiler_params=PARAMS,
         name="embed",
     )(
         me,
-        core,
         in_hbm(token_states),
         in_hbm(lengths.reshape(1, rows)),
         in_hbm(cluster_id.reshape(1, rows)),
@@ -146,42 +157,59 @@
     )(*blocks)
 
 
-def best_of(ref, columns, same):
-    scores = lax.dot_general(
-        ref[...], columns, (((1,), (1,)), ((), ())), preferred_element_type=jnp.float32
-    )
-    valid = ref[:, 0:LANES].astype(jnp.float32)[:, 0:1] < 1.5
-    if same:
-        valid = valid & (iota(scores.shape, 0) != iota(scores.shape, 1))
+def best_of(scores, rows):
+    valid = rows[:, 0:LANES].astype(jnp.float32)[:, 0:1] < 1.5
     return jnp.max(jnp.where(valid, scores, -1.0), axis=0, keepdims=True)
 
 
-def score_kernel(slot_cap, sources_of, me_ref, core_ref, mine_ref, other_ref, out_ref):
-    columns = mine_ref[...]
-    maxima = jnp.maximum(best_of(mine_ref, columns, True), best_of(other_ref, columns, False))
-    for at, source in enumerate(sources_of(out_ref.shape[0], me_ref, core_ref)):
+def inner_kernel(mine_ref, best_ref, turned_ref):
+    turned = mine_ref[...].T
+    turned_ref[...] = turned
+    scores = jnp.dot(mine_ref[...], turned, preferred_element_type=jnp.float32)
+    itself = iota(scores.shape, 0) == iota(scores.shape, 1)
+    best_ref[...] = best_of(jnp.where(itself, -1.0, scores), mine_ref)
+
+
+def inner_best(mine):
+    slots, width = mine.shape
+    return pl.pallas_call(
+        inner_kernel,
+        out_shape=(
+            jax.ShapeDtypeStruct((1, slots), jnp.float32),
+            jax.ShapeDtypeStruct((width, slots), mine.dtype),
+        ),
+        in_specs=[VMEM],
+        out_specs=(VMEM, VMEM),
+        compiler_params=PARAMS,
+        name="inner",
+    )(mine)
+
+
+def score_kernel(slot_cap, sources_of, me_ref, best_ref, turned_ref, other_ref, out_ref):
+    scores = jnp.dot(other_ref[...], turned_ref[...], preferred_element_type=jnp.float32)
+    maxima = jnp.maximum(best_ref[...], best_of(scores, other_ref))
+    for at, source in enumerate(sources_of(out_ref.shape[0], me_ref[0])):
         out_ref[source, :, 0:slot_cap] = maxima[:, at * slot_cap : (at + 1) * slot_cap]
 
 
-def order_sources(owners, me_ref, core_ref):
-    steps = [jnp.where(core_ref[0] == 0, *steps) for steps in zip(*ORDER)]
-    return [me_ref[0]] + [me_ref[0] ^ step for step in steps]
-
-
-def owner_sources(owners, *_):
+def order_sources(owners, me):
+    return [me] + [me ^ jnp.where(kind(me) == 0, *steps) for steps in zip(*ORDER)]
+
+
+def owner_sources(owners, _):
     return range(owners)
 
 
-def score(me, core, mine, other, owners, slot_cap, sources_of):
+def score(me, mine, other, owners, slot_cap, sources_of):
     lanes = -(-slot_cap // LANES) * LANES
     return pl.pallas_call(
         functools.partial(score_kernel, slot_cap, sources_of),
         out_shape=jax.ShapeDtypeStruct((owners, 1, lanes), jnp.float32),
-        in_specs=[SMEM] * 2 + [VMEM] * 2,
+        in_specs=[SMEM] + [VMEM] * 3,
         out_specs=VMEM,
         compiler_params=PARAMS,
         name="score",
-    )(me, core, mine, other)
+    )(me, *inner_best(mine), other)
 
 
 def pick_kernel(returned_ref, place_ref, out_ref):
@@ -206,14 +234,23 @@
     )(in_vmem(returned), in_vmem(place)).reshape(rows)
 
 
+def rows_of_devices(helpers, docs):
+    return [[doc * helpers + (row ^ turn(doc)) for doc in range(docs)] for row in range(helpers)]
+
+
 def step_to(value, steps):
-    helpers = lax.axis_size("help")
+    rows = rows_of_devices(lax.axis_size("help"), lax.axis_size("docs"))
     pairs = [
-        (doc * helpers + core, (doc ^ steps[core]) * helpers + core)
-        for doc in range(lax.axis_size("docs"))
-        for core in range(helpers)
+        (row[doc], row[doc ^ steps[kind(doc)]]) for row in rows for doc in range(len(row))
     ]
     return lax.ppermute(value, ("docs", "help"), pairs)
+
+
+def exchange(value):
+    rows = rows_of_devices(lax.axis_size("help"), lax.axis_size("docs"))
+    return lax.all_to_all(
+        value, ("docs", "help"), split_axis=0, concat_axis=0, tiled=True, axis_index_groups=rows
+    )
 
 
 def swap(value):
@@ -224,17 +261,16 @@
     owners = lax.axis_size("docs")
     slot_cap = 2 * arrays[0].shape[0] // owners
     me = lax.axis_index("docs").reshape(1)
-    core = lax.axis_index("help").reshape(1)
     if owners == len(ORDER[0]) + 1:
         block_of, sources_of = order_block, order_sources
-        own, *blocks, place = embed(me, core, arrays, [slot_cap] * owners, slot_cap, block_of)
+        own, *blocks, place = embed(me, arrays, [slot_cap] * owners, slot_cap, block_of)
         mine = join([own] + [step_to(*send) for send in zip(blocks, zip(*ORDER))])
     else:
         block_of, sources_of = owner_block, owner_sources
-        packed, place = embed(me, core, arrays, [owners * slot_cap], slot_cap, block_of)
-        mine = lax.all_to_all(packed, "docs", split_axis=0, concat_axis=0, tiled=True)
-    maxima = score(me, core, mine, swap(mine), owners, slot_cap, sources_of)
-    returned = lax.all_to_all(maxima, "docs", split_axis=0, concat_axis=0, tiled=True)
+        packed, place = embed(me, arrays, [owners * slot_cap], slot_cap, block_of)
+        mine = exchange(packed)
+    maxima = score(me, mine, swap(mine), owners, slot_cap, sources_of)
+    returned = exchange(maxima)
     return pick(returned, place)
 
 

time: 33.5 us -> 32.7 us (0.976)
  blocking collectives: 9.51 us -> 8.4 us
    all_to_all x1, blocking collectives: 9.51 us -> 8.4 us  [exchange(): lax.all_to_all(value, ('docs', 'help'), split_axis=0, concat_axis=0, tile...]
    ppermute x1, starting transfers between devices: 0.07 us -> 1.17 us  [swap(): lax.ppermute(value, 'help', [(i, i ^ 1) for i in range(lax.axis_size('hel...]
    ppermute x7, starting transfers between devices: 13.2 us -> 12.2 us  [step_to(): return lax.ppermute(value, ('docs', 'help'), pairs)]
    ppermute x1, waiting for transfers between devices: 1.9 us -> 1.13 us  [swap(): lax.ppermute(value, 'help', [(i, i ^ 1) for i in range(lax.axis_size('hel...]
    ppermute x7, waiting for transfers between devices: 4.81 us -> 5.45 us  [step_to(): return lax.ppermute(value, ('docs', 'help'), pairs)]
    pallas_call x0 -> x1, Pallas kernels: none -> 0.41 us  [inner_best(): pl.pallas_call(inner_kernel, out_shape=(jax.ShapeDtypeStruct((1, slots),...]
  transfers between devices with their start and end apart: 8 -> 8, of which waited for: 4 -> 5; matrix products, arithmetic and copies ran while one was open for 0% -> 0% of each run, Pallas kernels for 0% -> 1%
where the time goes in v4:
time: 32.7 us; the launch traced here: 32.5 us
  starting transfers between devices  13.4 us (41%)
  blocking collectives  8.4 us (26%)
  waiting for transfers between devices  6.58 us (20%)
  Pallas kernels  4.06 us (12%)
    ppermute x7, starting transfers between devices, step_to(): return lax.ppermute(value, ('docs', 'help'), pairs)  12.2 us
    all_to_all x1, blocking collectives, exchange(): lax.all_to_all(value, ('docs', 'help'), split_axis=0, concat_axis=0, tile...  8.4 us
    ppermute x7, waiting for transfers between devices, step_to(): return lax.ppermute(value, ('docs', 'help'), pairs)  5.45 us
    pallas_call x1, Pallas kernels, embed(): pl.pallas_call(functools.partial(embed_kernel, slot_cap, block_of), out_s...  2.63 us
    ppermute x1, starting transfers between devices, swap(): lax.ppermute(value, 'help', [(i, i ^ 1) for i in range(lax.axis_size('hel...  1.17 us
    ppermute x1, waiting for transfers between devices, swap(): lax.ppermute(value, 'help', [(i, i ^ 1) for i in range(lax.axis_size('hel...  1.13 us
  transfers between devices with their start and end apart: 8, of which 5 were waited for; matrix products, arithmetic and copies ran while one was open for 0% of the time, Pallas kernels for 1%

profile of v4, /device:TPU:0, one launch (start us, length us, event | category | flops | bytes accessed | tf_op | source)
XLA Modules:
  0.0 32.5 jit_solution(3251238687291685391)
XLA Ops:
  0.0 2.6 %embed.1 = (bf16[32,1024]{1,0:T(8,128)(2,1)S(1)}, bf16[32,1024]{1,0:T(8,128)(2,1)S(1)}, bf16[32,1024]{1,0:T(8,128)(2,1)S(1)}, bf16[32,1024]{1,0:T(8,128)(2,1)S(1...) custom-call(s32[1]{0:T(128)} %bitcast.me_ref, ...), custom_call_target="tpu_custom_call" | custom-call | tf_op jit(solution)/shard_map/embed/pallas_call | solution.py:114
  2.6 4.5 %collective-permute-start = (bf16[32,1024]{1,0:T(8,128)(2,1)S(1)}, bf16[32,1024]{1,0:T(8,128)(2,1)S(1)}, u32[]{:S(2)}, u32[]{:S(2)}) collective-permute-start(bf16[32,1024]{1,0:T(8,128)(2,1)S(1)} %get-tuple-element.17), channel_id=1, source_target_pairs={{0,13},{2,15},{4,9},{6,11},{9,4},{11,6},{13,0},{15,2},{1,12},{3,14... | collective-permute-start | bytes 196616 | tf_op jit(solution)/shard_map/ppermute | solution.py:246
  7.2 1.5 %collective-permute-start.1 = (bf16[32,1024]{1,0:T(8,128)(2,1)S(1)}, bf16[32,1024]{1,0:T(8,128)(2,1)S(1)}, u32[]{:S(2)}, u32[]{:S(2)}) collective-permute-start(bf16[32,1024]{1,0:T(8,128)(2,1)S(1)} %get-tuple-element.18), channel_id=1, source_target_pairs={{0,2},{2,0},{4,6},{6,4},{9,11},{11,9},{13,15},{15,13},{1,3},{3,1},... | collective-permute-start | bytes 196616 | tf_op jit(solution)/shard_map/ppermute | solution.py:246
  8.7 0.0 collective-permute-start.2
  8.7 0.0 collective-permute-start.3
  8.7 3.8 %collective-permute-start.4 = (bf16[32,1024]{1,0:T(8,128)(2,1)S(1)}, bf16[32,1024]{1,0:T(8,128)(2,1)S(1)}, u32[]{:S(2)}, u32[]{:S(2)}) collective-permute-start(bf16[32,1024]{1,0:T(8,128)(2,1)S(1)} %get-tuple-element.21), channel_id=1, source_target_pairs={{0,9},{2,11},{4,13},{6,15},{9,0},{11,2},{13,4},{15,6},{1,8},{3,10}... | collective-permute-start | bytes 196616 | tf_op jit(solution)/shard_map/ppermute | solution.py:246
  12.5 0.0 collective-permute-done.refs_1_
  12.5 1.3 %collective-permute-start.5 = (bf16[32,1024]{1,0:T(8,128)(2,1)S(1)}, bf16[32,1024]{1,0:T(8,128)(2,1)S(1)}, u32[]{:S(2)}, u32[]{:S(2)}) collective-permute-start(bf16[32,1024]{1,0:T(8,128)(2,1)S(1)} %get-tuple-element.22), channel_id=1, source_target_pairs={{0,6},{2,4},{4,2},{6,0},{9,15},{11,13},{13,11},{15,9},{1,7},{3,5},... | collective-permute-start | bytes 196616 | tf_op jit(solution)/shard_map/ppermute | solution.py:246
  13.7 0.0 collective-permute-done.1.refs_2_
  13.8 1.1 %collective-permute-start.6 = (bf16[32,1024]{1,0:T(8,128)(2,1)S(1)}, bf16[32,1024]{1,0:T(8,128)(2,1)S(1)}, u32[]{:S(2)}, u32[]{:S(2)}) collective-permute-start(bf16[32,1024]{1,0:T(8,128)(2,1)S(1)} %get-tuple-element.23), channel_id=1, source_target_pairs={{0,11},{2,9},{4,15},{6,13},{9,2},{11,0},{13,6},{15,4},{1,10},{3,8}... | collective-permute-start | bytes 196616 | tf_op jit(solution)/shard_map/ppermute | solution.py:246
  14.9 0.5 %collective-permute-done.2.refs_3_ = bf16[32,1024]{1,0:T(8,128)(2,1)S(1)} collective-permute-done((bf16[32,1024]{1,0:T(8,128)(2,1)S(1)}, bf16[32,1024]{1,0:T(8,128)(2,1)S(1)}, u32[]{:S(2)}, u32[]{:S(2)}) %collective-permute-start.2) | collective-permute-done | bytes 65568 | tf_op jit(solution)/shard_map/ppermute | solution.py:246
  15.4 0.0 collective-permute-done.3.refs_4_
  15.4 1.1 %collective-permute-done.4.refs_5_ = bf16[32,1024]{1,0:T(8,128)(2,1)S(1)} collective-permute-done((bf16[32,1024]{1,0:T(8,128)(2,1)S(1)}, bf16[32,1024]{1,0:T(8,128)(2,1)S(1)}, u32[]{:S(2)}, u32[]{:S(2)}) %collective-permute-start.4) | collective-permute-done | bytes 65568 | tf_op jit(solution)/shard_map/ppermute | solution.py:246
  16.5 2.2 %collective-permute-done.5.refs_6_ = bf16[32,1024]{1,0:T(8,128)(2,1)S(1)} collective-permute-done((bf16[32,1024]{1,0:T(8,128)(2,1)S(1)}, bf16[32,1024]{1,0:T(8,128)(2,1)S(1)}, u32[]{:S(2)}, u32[]{:S(2)}) %collective-permute-start.5) | collective-permute-done | bytes 65568 | tf_op jit(solution)/shard_map/ppermute | solution.py:246
  18.7 1.6 %collective-permute-done.6.refs_7_ = bf16[32,1024]{1,0:T(8,128)(2,1)S(1)} collective-permute-done((bf16[32,1024]{1,0:T(8,128)(2,1)S(1)}, bf16[32,1024]{1,0:T(8,128)(2,1)S(1)}, u32[]{:S(2)}, u32[]{:S(2)}) %collective-permute-start.6) | collective-permute-done | bytes 65568 | tf_op jit(solution)/shard_map/ppermute | solution.py:246
  20.4 1.2 %collective-permute-start.7 = (bf16[256,1024]{1,0:T(8,128)(2,1)S(1)}, bf16[256,1024]{1,0:T(8,128)(2,1)S(1)}, u32[]{:S(2)}, u32[]{:S(2)}) collective-permute-start(bf16[256,1024]{1,0:T(8,128)(2,1)S(1)} %join.1.mine_ref), channel_id=1, source_target_pairs={{0,1},{1,0},{2,3},{3,2},{4,5},{5,4},{6,7},{7,6},{8,9},{9,8},{10,11... | collective-permute-start | bytes 1572872 | tf_op jit(solution)/shard_map/ppermute | solution.py:257
  21.6 0.4 %inner.1 = (f32[1,256]{1,0:T(1,128)S(1)}, bf16[1024,256]{1,0:T(8,128)(2,1)S(1)}) custom-call(bf16[256,1024]{1,0:T(8,128)(2,1)S(1)} %join.1.mine_ref), custom_call_target="tpu_custom_call" | custom-call | tf_op jit(solution)/shard_map/inner/pallas_call | solution.py:175
  22.0 1.1 %collective-permute-done.7.other_ref = bf16[256,1024]{1,0:T(8,128)(2,1)S(1)} collective-permute-done((bf16[256,1024]{1,0:T(8,128)(2,1)S(1)}, bf16[256,1024]{1,0:T(8,128)(2,1)S(1)}, u32[]{:S(2)}, u32[]{:S(2)}) %collective-permute-start.7) | collective-permute-done | bytes 524320 | tf_op jit(solution)/shard_map/ppermute | solution.py:257
  23.1 0.4 %score.1 = f32[8,1,128]{2,1,0:T(1,128)S(1)} custom-call(s32[1]{0:T(128)} %bitcast.me_ref, f32[1,256]{1,0:T(1,128)S(1)} %get-tuple-element.24.best_ref, bf16[1024,256]{1,0:T(8,128)(2,1)S(1)} %get-tuple-element.25.turned_ref, bf16[256,1024]{1,0:T(8,128)(2,1)S(1)} %collective-permute-done.7.other_ref), custom_call_target="tpu_custom_call" | custom-call | tf_op jit(solution)/shard_map/score/pallas_call | solution.py:205
  23.5 8.4 %all_to_all.5.returned_ref = f32[8,1,128]{2,1,0:T(1,128)S(1)} all-to-all(f32[8,1,128]{2,1,0:T(1,128)S(1)} %score.1), channel_id=1, replica_groups={{0,2,4,6,9,11,13,15},{1,3,5,7,8,10,12,14},{16,18,20,22,25,27,29,31},{17..., dimensions={0} | all-to-all | bytes 8192 | tf_op jit(solution)/shard_map/all_to_all | solution.py:251
  31.9 0.6 %pick.1 = f32[1,128]{1,0:T(1,128)} custom-call(f32[8,1,128]{2,1,0:T(1,128)S(1)} %all_to_all.5.returned_ref, s32[8,128]{1,0:T(8,128)S(1)} %get-tuple-element.26.place_ref), custom_call_target="tpu_custom_call" | custom-call | tf_op jit(solution)/shard_map/pick/pallas_call | solution.py:228
  (1 shorter events, 0.0 us)
Async XLA Ops:
  2.6 9.8 %collective-permute-start = (bf16[32,1024]{1,0:T(8,128)(2,1)S(1)}, bf16[32,1024]{1,0:T(8,128)(2,1)S(1)}, u32[]{:S(2)}, u32[]{:S(2)}) collective-permute-start(bf16[32,1024]{1,0:T(8,128)(2,1)S(1)} %get-tuple-element.17), channel_id=1, source_target_pairs={{0,13},{2,15},{4,9},{6,11},{9,4},{11,6},{13,0},{15,2},{1,12},{3,14... | collective-permute-start | bytes 196616 | tf_op jit(solution)/shard_map/ppermute | solution.py:246
  7.2 6.6 %collective-permute-start.1 = (bf16[32,1024]{1,0:T(8,128)(2,1)S(1)}, bf16[32,1024]{1,0:T(8,128)(2,1)S(1)}, u32[]{:S(2)}, u32[]{:S(2)}) collective-permute-start(bf16[32,1024]{1,0:T(8,128)(2,1)S(1)} %get-tuple-element.18), channel_id=1, source_target_pairs={{0,2},{2,0},{4,6},{6,4},{9,11},{11,9},{13,15},{15,13},{1,3},{3,1},... | collective-permute-start | bytes 196616 | tf_op jit(solution)/shard_map/ppermute | solution.py:246
  8.7 6.7 %collective-permute-start.2 = (bf16[32,1024]{1,0:T(8,128)(2,1)S(1)}, bf16[32,1024]{1,0:T(8,128)(2,1)S(1)}, u32[]{:S(2)}, u32[]{:S(2)}) collective-permute-start(bf16[32,1024]{1,0:T(8,128)(2,1)S(1)} %get-tuple-element.19), channel_id=1, source_target_pairs={{0,15},{2,13},{4,11},{6,9},{9,6},{11,4},{13,2},{15,0},{1,14},{3,12... | collective-permute-start | bytes 196616 | tf_op jit(solution)/shard_map/ppermute | solution.py:246
  8.7 6.7 %collective-permute-start.3 = (bf16[32,1024]{1,0:T(8,128)(2,1)S(1)}, bf16[32,1024]{1,0:T(8,128)(2,1)S(1)}, u32[]{:S(2)}, u32[]{:S(2)}) collective-permute-start(bf16[32,1024]{1,0:T(8,128)(2,1)S(1)} %get-tuple-element.20), channel_id=1, source_target_pairs={{0,4},{2,6},{4,0},{6,2},{9,13},{11,15},{13,9},{15,11},{1,5},{3,7},... | collective-permute-start | bytes 196616 | tf_op jit(solution)/shard_map/ppermute | solution.py:246
  8.7 7.8 %collective-permute-start.4 = (bf16[32,1024]{1,0:T(8,128)(2,1)S(1)}, bf16[32,1024]{1,0:T(8,128)(2,1)S(1)}, u32[]{:S(2)}, u32[]{:S(2)}) collective-permute-start(bf16[32,1024]{1,0:T(8,128)(2,1)S(1)} %get-tuple-element.21), channel_id=1, source_target_pairs={{0,9},{2,11},{4,13},{6,15},{9,0},{11,2},{13,4},{15,6},{1,8},{3,10}... | collective-permute-start | bytes 196616 | tf_op jit(solution)/shard_map/ppermute | solution.py:246
  12.5 6.2 %collective-permute-start.5 = (bf16[32,1024]{1,0:T(8,128)(2,1)S(1)}, bf16[32,1024]{1,0:T(8,128)(2,1)S(1)}, u32[]{:S(2)}, u32[]{:S(2)}) collective-permute-start(bf16[32,1024]{1,0:T(8,128)(2,1)S(1)} %get-tuple-element.22), channel_id=1, source_target_pairs={{0,6},{2,4},{4,2},{6,0},{9,15},{11,13},{13,11},{15,9},{1,7},{3,5},... | collective-permute-start | bytes 196616 | tf_op jit(solution)/shard_map/ppermute | solution.py:246
  13.8 6.6 %collective-permute-start.6 = (bf16[32,1024]{1,0:T(8,128)(2,1)S(1)}, bf16[32,1024]{1,0:T(8,128)(2,1)S(1)}, u32[]{:S(2)}, u32[]{:S(2)}) collective-permute-start(bf16[32,1024]{1,0:T(8,128)(2,1)S(1)} %get-tuple-element.23), channel_id=1, source_target_pairs={{0,11},{2,9},{4,15},{6,13},{9,2},{11,0},{13,6},{15,4},{1,10},{3,8}... | collective-permute-start | bytes 196616 | tf_op jit(solution)/shard_map/ppermute | solution.py:246
  20.4 2.7 %collective-permute-start.7 = (bf16[256,1024]{1,0:T(8,128)(2,1)S(1)}, bf16[256,1024]{1,0:T(8,128)(2,1)S(1)}, u32[]{:S(2)}, u32[]{:S(2)}) collective-permute-start(bf16[256,1024]{1,0:T(8,128)(2,1)S(1)} %join.1.mine_ref), channel_id=1, source_target_pairs={{0,1},{1,0},{2,3},{3,2},{4,5},{5,4},{6,7},{7,6},{8,9},{9,8},{10,11... | collective-permute-start | bytes 1572872 | tf_op jit(solution)/shard_map/ppermute | solution.py:257

commit v5 on v4

--- a/solution.py
+++ b/solution.py
@@ -16,15 +16,11 @@
 HBM = pl.BlockSpec(memory_space=pltpu.HBM)
 PARAMS = pltpu.CompilerParams(vmem_limit_bytes=32 * 2**20)
 
-ORDER = ((6, 1, 7, 2, 4, 3, 5), (6, 1, 7, 2, 4, 3, 5))
+ORDER = (6, 1, 7, 2, 5, 3, 4)
 
 
 def turn(doc):
     return (doc >> 2) & 1
-
-
-def kind(doc):
-    return ((doc >> 1) ^ (doc >> 2)) & 1
 
 
 def iota(shape, dim):
@@ -99,8 +95,8 @@
 def order_block(owner, me):
     step = owner ^ me
     block = jnp.zeros_like(step)
-    for at, steps in enumerate(zip(*ORDER), 1):
-        block = jnp.where(step == jnp.where(kind(me) == 0, *steps), at, block)
+    for at, other in enumerate(ORDER, 1):
+        block = jnp.where(step == other, at, block)
     return block
 
 
@@ -193,7 +189,7 @@
 
 
 def order_sources(owners, me):
-    return [me] + [me ^ jnp.where(kind(me) == 0, *steps) for steps in zip(*ORDER)]
+    return [me] + [me ^ step for step in ORDER]
 
 
 def owner_sources(owners, _):
@@ -238,11 +234,9 @@
     return [[doc * helpers + (row ^ turn(doc)) for doc in range(docs)] for row in range(helpers)]
 
 
-def step_to(value, steps):
+def step_to(value, step):
     rows = rows_of_devices(lax.axis_size("help"), lax.axis_size("docs"))
-    pairs = [
-        (row[doc], row[doc ^ steps[kind(doc)]]) for row in rows for doc in range(len(row))
-    ]
+    pairs = [(row[doc], row[doc ^ step]) for row in rows for doc in range(len(row))]
     return lax.ppermute(value, ("docs", "help"), pairs)
 
 
@@ -261,10 +255,10 @@
     owners = lax.axis_size("docs")
     slot_cap = 2 * arrays[0].shape[0] // owners
     me = lax.axis_index("docs").reshape(1)
-    if owners == len(ORDER[0]) + 1:
+    if owners == len(ORDER) + 1:
         block_of, sources_of = order_block, order_sources
         own, *blocks, place = embed(me, arrays, [slot_cap] * owners, slot_cap, block_of)
-        mine = join([own] + [step_to(*send) for send in zip(blocks, zip(*ORDER))])
+        mine = join([own] + [step_to(*send) for send in zip(blocks, ORDER)])
     else:
         block_of, sources_of = owner_block, owner_sources
         packed, place = embed(me, arrays, [owners * slot_cap], slot_cap, block_of)

time: 32.7 us -> 32.3 us (0.988)
  starting transfers between devices: 13.4 us -> 12.6 us
  blocking collectives: 8.4 us -> 8.87 us
    ppermute x1, starting transfers between devices: 1.17 us -> 0.34 us  [swap(): lax.ppermute(value, 'help', [(i, i ^ 1) for i in range(lax.axis_size('hel...]
    all_to_all x1, blocking collectives: 8.4 us -> 8.87 us  [exchange(): lax.all_to_all(value, ('docs', 'help'), split_axis=0, concat_axis=0, tile...]
  transfers between devices with their start and end apart: 8 -> 8, of which waited for: 5 -> 4; matrix products, arithmetic and copies ran while one was open for 0% -> 0% of each run, Pallas kernels for 1% -> 1%
where the time goes in v5:
time: 32.3 us; the launch traced here: 32.1 us
  starting transfers between devices  12.6 us (39%)
  blocking collectives  8.87 us (27%)
  waiting for transfers between devices  6.55 us (20%)
  Pallas kernels  4.07 us (13%)
    ppermute x7, starting transfers between devices, step_to(): return lax.ppermute(value, ('docs', 'help'), pairs)  12.3 us
    all_to_all x1, blocking collectives, exchange(): lax.all_to_all(value, ('docs', 'help'), split_axis=0, concat_axis=0, tile...  8.87 us
    ppermute x7, waiting for transfers between devices, step_to(): return lax.ppermute(value, ('docs', 'help'), pairs)  5.33 us
    pallas_call x1, Pallas kernels, embed(): pl.pallas_call(functools.partial(embed_kernel, slot_cap, block_of), out_s...  2.63 us
    ppermute x1, waiting for transfers between devices, swap(): lax.ppermute(value, 'help', [(i, i ^ 1) for i in range(lax.axis_size('hel...  1.22 us
  transfers between devices with their start and end apart: 8, of which 4 were waited for; matrix products, arithmetic and copies ran while one was open for 0% of the time, Pallas kernels for 1%

profile of v5, /device:TPU:0, one launch (start us, length us, event | category | flops | bytes accessed | tf_op | source)
XLA Modules:
  0.0 32.1 jit_solution(9342266915893465865)
XLA Ops:
  0.0 2.6 %embed.1 = (bf16[32,1024]{1,0:T(8,128)(2,1)S(1)}, bf16[32,1024]{1,0:T(8,128)(2,1)S(1)}, bf16[32,1024]{1,0:T(8,128)(2,1)S(1)}, bf16[32,1024]{1,0:T(8,128)(2,1)S(1...) custom-call(s32[1]{0:T(128)} %bitcast.me_ref, ...), custom_call_target="tpu_custom_call" | custom-call | tf_op jit(solution)/shard_map/embed/pallas_call | solution.py:110
  2.6 4.5 %collective-permute-start = (bf16[32,1024]{1,0:T(8,128)(2,1)S(1)}, bf16[32,1024]{1,0:T(8,128)(2,1)S(1)}, u32[]{:S(2)}, u32[]{:S(2)}) collective-permute-start(bf16[32,1024]{1,0:T(8,128)(2,1)S(1)} %get-tuple-element.17), channel_id=1, source_target_pairs={{0,13},{2,15},{4,9},{6,11},{9,4},{11,6},{13,0},{15,2},{1,12},{3,14... | collective-permute-start | bytes 196616 | tf_op jit(solution)/shard_map/ppermute | solution.py:240
  7.2 1.5 %collective-permute-start.1 = (bf16[32,1024]{1,0:T(8,128)(2,1)S(1)}, bf16[32,1024]{1,0:T(8,128)(2,1)S(1)}, u32[]{:S(2)}, u32[]{:S(2)}) collective-permute-start(bf16[32,1024]{1,0:T(8,128)(2,1)S(1)} %get-tuple-element.18), channel_id=1, source_target_pairs={{0,2},{2,0},{4,6},{6,4},{9,11},{11,9},{13,15},{15,13},{1,3},{3,1},... | collective-permute-start | bytes 196616 | tf_op jit(solution)/shard_map/ppermute | solution.py:240
  8.7 0.0 collective-permute-start.2
  8.7 0.0 collective-permute-start.3
  8.7 4.8 %collective-permute-start.4 = (bf16[32,1024]{1,0:T(8,128)(2,1)S(1)}, bf16[32,1024]{1,0:T(8,128)(2,1)S(1)}, u32[]{:S(2)}, u32[]{:S(2)}) collective-permute-start(bf16[32,1024]{1,0:T(8,128)(2,1)S(1)} %get-tuple-element.21), channel_id=1, source_target_pairs={{0,11},{2,9},{4,15},{6,13},{9,2},{11,0},{13,6},{15,4},{1,10},{3,8}... | collective-permute-start | bytes 196616 | tf_op jit(solution)/shard_map/ppermute | solution.py:240
  13.4 0.0 collective-permute-done.refs_1_
  13.5 0.2 collective-permute-start.5
  13.7 0.0 collective-permute-done.1.refs_2_
  13.7 1.2 %collective-permute-start.6 = (bf16[32,1024]{1,0:T(8,128)(2,1)S(1)}, bf16[32,1024]{1,0:T(8,128)(2,1)S(1)}, u32[]{:S(2)}, u32[]{:S(2)}) collective-permute-start(bf16[32,1024]{1,0:T(8,128)(2,1)S(1)} %get-tuple-element.23), channel_id=1, source_target_pairs={{0,9},{2,11},{4,13},{6,15},{9,0},{11,2},{13,4},{15,6},{1,8},{3,10}... | collective-permute-start | bytes 196616 | tf_op jit(solution)/shard_map/ppermute | solution.py:240
  14.9 0.5 %collective-permute-done.2.refs_3_ = bf16[32,1024]{1,0:T(8,128)(2,1)S(1)} collective-permute-done((bf16[32,1024]{1,0:T(8,128)(2,1)S(1)}, bf16[32,1024]{1,0:T(8,128)(2,1)S(1)}, u32[]{:S(2)}, u32[]{:S(2)}) %collective-permute-start.2) | collective-permute-done | bytes 65568 | tf_op jit(solution)/shard_map/ppermute | solution.py:240
  15.4 0.0 collective-permute-done.3.refs_4_
  15.4 2.1 %collective-permute-done.4.refs_5_ = bf16[32,1024]{1,0:T(8,128)(2,1)S(1)} collective-permute-done((bf16[32,1024]{1,0:T(8,128)(2,1)S(1)}, bf16[32,1024]{1,0:T(8,128)(2,1)S(1)}, u32[]{:S(2)}, u32[]{:S(2)}) %collective-permute-start.4) | collective-permute-done | bytes 65568 | tf_op jit(solution)/shard_map/ppermute | solution.py:240
  17.5 2.7 %collective-permute-done.5.refs_6_ = bf16[32,1024]{1,0:T(8,128)(2,1)S(1)} collective-permute-done((bf16[32,1024]{1,0:T(8,128)(2,1)S(1)}, bf16[32,1024]{1,0:T(8,128)(2,1)S(1)}, u32[]{:S(2)}, u32[]{:S(2)}) %collective-permute-start.5) | collective-permute-done | bytes 65568 | tf_op jit(solution)/shard_map/ppermute | solution.py:240
  20.2 0.0 collective-permute-done.6.refs_7_
  20.3 0.3 %collective-permute-start.7 = (bf16[256,1024]{1,0:T(8,128)(2,1)S(1)}, bf16[256,1024]{1,0:T(8,128)(2,1)S(1)}, u32[]{:S(2)}, u32[]{:S(2)}) collective-permute-start(bf16[256,1024]{1,0:T(8,128)(2,1)S(1)} %join.1.mine_ref), channel_id=1, source_target_pairs={{0,1},{1,0},{2,3},{3,2},{4,5},{5,4},{6,7},{7,6},{8,9},{9,8},{10,11... | collective-permute-start | bytes 1572872 | tf_op jit(solution)/shard_map/ppermute | solution.py:251
  20.6 0.4 %inner.1 = (f32[1,256]{1,0:T(1,128)S(1)}, bf16[1024,256]{1,0:T(8,128)(2,1)S(1)}) custom-call(bf16[256,1024]{1,0:T(8,128)(2,1)S(1)} %join.1.mine_ref), custom_call_target="tpu_custom_call" | custom-call | tf_op jit(solution)/shard_map/inner/pallas_call | solution.py:171
  21.0 1.2 %collective-permute-done.7.other_ref = bf16[256,1024]{1,0:T(8,128)(2,1)S(1)} collective-permute-done((bf16[256,1024]{1,0:T(8,128)(2,1)S(1)}, bf16[256,1024]{1,0:T(8,128)(2,1)S(1)}, u32[]{:S(2)}, u32[]{:S(2)}) %collective-permute-start.7) | collective-permute-done | bytes 524320 | tf_op jit(solution)/shard_map/ppermute | solution.py:251
  22.3 0.4 %score.1 = f32[8,1,128]{2,1,0:T(1,128)S(1)} custom-call(s32[1]{0:T(128)} %bitcast.me_ref, f32[1,256]{1,0:T(1,128)S(1)} %get-tuple-element.24.best_ref, bf16[1024,256]{1,0:T(8,128)(2,1)S(1)} %get-tuple-element.25.turned_ref, bf16[256,1024]{1,0:T(8,128)(2,1)S(1)} %collective-permute-done.7.other_ref), custom_call_target="tpu_custom_call" | custom-call | tf_op jit(solution)/shard_map/score/pallas_call | solution.py:201
  22.6 8.9 %all_to_all.5.returned_ref = f32[8,1,128]{2,1,0:T(1,128)S(1)} all-to-all(f32[8,1,128]{2,1,0:T(1,128)S(1)} %score.1), channel_id=1, replica_groups={{0,2,4,6,9,11,13,15},{1,3,5,7,8,10,12,14},{16,18,20,22,25,27,29,31},{17..., dimensions={0} | all-to-all | bytes 8192 | tf_op jit(solution)/shard_map/all_to_all | solution.py:245
  31.5 0.6 %pick.1 = f32[1,128]{1,0:T(1,128)} custom-call(f32[8,1,128]{2,1,0:T(1,128)S(1)} %all_to_all.5.returned_ref, s32[8,128]{1,0:T(8,128)S(1)} %get-tuple-element.26.place_ref), custom_call_target="tpu_custom_call" | custom-call | tf_op jit(solution)/shard_map/pick/pallas_call | solution.py:224
  (1 shorter events, 0.0 us)
Async XLA Ops:
  2.6 10.8 %collective-permute-start = (bf16[32,1024]{1,0:T(8,128)(2,1)S(1)}, bf16[32,1024]{1,0:T(8,128)(2,1)S(1)}, u32[]{:S(2)}, u32[]{:S(2)}) collective-permute-start(bf16[32,1024]{1,0:T(8,128)(2,1)S(1)} %get-tuple-element.17), channel_id=1, source_target_pairs={{0,13},{2,15},{4,9},{6,11},{9,4},{11,6},{13,0},{15,2},{1,12},{3,14... | collective-permute-start | bytes 196616 | tf_op jit(solution)/shard_map/ppermute | solution.py:240
  7.2 6.5 %collective-permute-start.1 = (bf16[32,1024]{1,0:T(8,128)(2,1)S(1)}, bf16[32,1024]{1,0:T(8,128)(2,1)S(1)}, u32[]{:S(2)}, u32[]{:S(2)}) collective-permute-start(bf16[32,1024]{1,0:T(8,128)(2,1)S(1)} %get-tuple-element.18), channel_id=1, source_target_pairs={{0,2},{2,0},{4,6},{6,4},{9,11},{11,9},{13,15},{15,13},{1,3},{3,1},... | collective-permute-start | bytes 196616 | tf_op jit(solution)/shard_map/ppermute | solution.py:240
  8.7 6.7 %collective-permute-start.2 = (bf16[32,1024]{1,0:T(8,128)(2,1)S(1)}, bf16[32,1024]{1,0:T(8,128)(2,1)S(1)}, u32[]{:S(2)}, u32[]{:S(2)}) collective-permute-start(bf16[32,1024]{1,0:T(8,128)(2,1)S(1)} %get-tuple-element.19), channel_id=1, source_target_pairs={{0,15},{2,13},{4,11},{6,9},{9,6},{11,4},{13,2},{15,0},{1,14},{3,12... | collective-permute-start | bytes 196616 | tf_op jit(solution)/shard_map/ppermute | solution.py:240
  8.7 6.7 %collective-permute-start.3 = (bf16[32,1024]{1,0:T(8,128)(2,1)S(1)}, bf16[32,1024]{1,0:T(8,128)(2,1)S(1)}, u32[]{:S(2)}, u32[]{:S(2)}) collective-permute-start(bf16[32,1024]{1,0:T(8,128)(2,1)S(1)} %get-tuple-element.20), channel_id=1, source_target_pairs={{0,4},{2,6},{4,0},{6,2},{9,13},{11,15},{13,9},{15,11},{1,5},{3,7},... | collective-permute-start | bytes 196616 | tf_op jit(solution)/shard_map/ppermute | solution.py:240
  8.7 8.8 %collective-permute-start.4 = (bf16[32,1024]{1,0:T(8,128)(2,1)S(1)}, bf16[32,1024]{1,0:T(8,128)(2,1)S(1)}, u32[]{:S(2)}, u32[]{:S(2)}) collective-permute-start(bf16[32,1024]{1,0:T(8,128)(2,1)S(1)} %get-tuple-element.21), channel_id=1, source_target_pairs={{0,11},{2,9},{4,15},{6,13},{9,2},{11,0},{13,6},{15,4},{1,10},{3,8}... | collective-permute-start | bytes 196616 | tf_op jit(solution)/shard_map/ppermute | solution.py:240
  13.5 6.8 %collective-permute-start.5 = (bf16[32,1024]{1,0:T(8,128)(2,1)S(1)}, bf16[32,1024]{1,0:T(8,128)(2,1)S(1)}, u32[]{:S(2)}, u32[]{:S(2)}) collective-permute-start(bf16[32,1024]{1,0:T(8,128)(2,1)S(1)} %get-tuple-element.22), channel_id=1, source_target_pairs={{0,6},{2,4},{4,2},{6,0},{9,15},{11,13},{13,11},{15,9},{1,7},{3,5},... | collective-permute-start | bytes 196616 | tf_op jit(solution)/shard_map/ppermute | solution.py:240
  13.7 6.6 %collective-permute-start.6 = (bf16[32,1024]{1,0:T(8,128)(2,1)S(1)}, bf16[32,1024]{1,0:T(8,128)(2,1)S(1)}, u32[]{:S(2)}, u32[]{:S(2)}) collective-permute-start(bf16[32,1024]{1,0:T(8,128)(2,1)S(1)} %get-tuple-element.23), channel_id=1, source_target_pairs={{0,9},{2,11},{4,13},{6,15},{9,0},{11,2},{13,4},{15,6},{1,8},{3,10}... | collective-permute-start | bytes 196616 | tf_op jit(solution)/shard_map/ppermute | solution.py:240
  20.3 2.0 %collective-permute-start.7 = (bf16[256,1024]{1,0:T(8,128)(2,1)S(1)}, bf16[256,1024]{1,0:T(8,128)(2,1)S(1)}, u32[]{:S(2)}, u32[]{:S(2)}) collective-permute-start(bf16[256,1024]{1,0:T(8,128)(2,1)S(1)} %join.1.mine_ref), channel_id=1, source_target_pairs={{0,1},{1,0},{2,3},{3,2},{4,5},{5,4},{6,7},{7,6},{8,9},{9,8},{10,11... | collective-permute-start | bytes 1572872 | tf_op jit(solution)/shard_map/ppermute | solution.py:251

commit v6 on v5

--- a/solution.py
+++ b/solution.py
@@ -10,7 +10,7 @@
 CL_OWN = 1
 LANES = 128
 EMPTY = 2.0
-WEIGHT_PARTS = 8
+WEIGHT_PARTS = 4
 VMEM = pl.BlockSpec(memory_space=pltpu.VMEM)
 SMEM = pl.BlockSpec(memory_space=pltpu.SMEM)
 HBM = pl.BlockSpec(memory_space=pltpu.HBM)

time: 32.3 us -> 32.1 us (level)
  no operation moved by 1% of the time
where the time goes in v6:
time: 32.1 us; the launch traced here: 32 us
  starting transfers between devices  12.6 us (39%)
  blocking collectives  8.73 us (27%)
  waiting for transfers between devices  6.58 us (20%)
  Pallas kernels  4.05 us (13%)
    ppermute x7, starting transfers between devices, step_to(): return lax.ppermute(value, ('docs', 'help'), pairs)  12.3 us
    all_to_all x1, blocking collectives, exchange(): lax.all_to_all(value, ('docs', 'help'), split_axis=0, concat_axis=0, tile...  8.73 us
    ppermute x7, waiting for transfers between devices, step_to(): return lax.ppermute(value, ('docs', 'help'), pairs)  5.34 us
    pallas_call x1, Pallas kernels, embed(): pl.pallas_call(functools.partial(embed_kernel, slot_cap, block_of), out_s...  2.61 us
    ppermute x1, waiting for transfers between devices, swap(): lax.ppermute(value, 'help', [(i, i ^ 1) for i in range(lax.axis_size('hel...  1.24 us
  transfers between devices with their start and end apart: 8, of which 4 were waited for; matrix products, arithmetic and copies ran while one was open for 0% of the time, Pallas kernels for 1%

profile of v6, /device:TPU:0, one launch (start us, length us, event | category | flops | bytes accessed | tf_op | source)
XLA Modules:
  0.0 32.0 jit_solution(15754430260775130914)
XLA Ops:
  0.0 2.6 %embed.1 = (bf16[32,1024]{1,0:T(8,128)(2,1)S(1)}, bf16[32,1024]{1,0:T(8,128)(2,1)S(1)}, bf16[32,1024]{1,0:T(8,128)(2,1)S(1)}, bf16[32,1024]{1,0:T(8,128)(2,1)S(1...) custom-call(s32[1]{0:T(128)} %bitcast.me_ref, ...), custom_call_target="tpu_custom_call" | custom-call | tf_op jit(solution)/shard_map/embed/pallas_call | solution.py:110
  2.6 4.6 %collective-permute-start = (bf16[32,1024]{1,0:T(8,128)(2,1)S(1)}, bf16[32,1024]{1,0:T(8,128)(2,1)S(1)}, u32[]{:S(2)}, u32[]{:S(2)}) collective-permute-start(bf16[32,1024]{1,0:T(8,128)(2,1)S(1)} %get-tuple-element.17), channel_id=1, source_target_pairs={{0,13},{2,15},{4,9},{6,11},{9,4},{11,6},{13,0},{15,2},{1,12},{3,14... | collective-permute-start | bytes 196616 | tf_op jit(solution)/shard_map/ppermute | solution.py:240
  7.2 1.5 %collective-permute-start.1 = (bf16[32,1024]{1,0:T(8,128)(2,1)S(1)}, bf16[32,1024]{1,0:T(8,128)(2,1)S(1)}, u32[]{:S(2)}, u32[]{:S(2)}) collective-permute-start(bf16[32,1024]{1,0:T(8,128)(2,1)S(1)} %get-tuple-element.18), channel_id=1, source_target_pairs={{0,2},{2,0},{4,6},{6,4},{9,11},{11,9},{13,15},{15,13},{1,3},{3,1},... | collective-permute-start | bytes 196616 | tf_op jit(solution)/shard_map/ppermute | solution.py:240
  8.7 0.0 collective-permute-start.2
  8.7 0.0 collective-permute-start.3
  8.7 4.7 %collective-permute-start.4 = (bf16[32,1024]{1,0:T(8,128)(2,1)S(1)}, bf16[32,1024]{1,0:T(8,128)(2,1)S(1)}, u32[]{:S(2)}, u32[]{:S(2)}) collective-permute-start(bf16[32,1024]{1,0:T(8,128)(2,1)S(1)} %get-tuple-element.21), channel_id=1, source_target_pairs={{0,11},{2,9},{4,15},{6,13},{9,2},{11,0},{13,6},{15,4},{1,10},{3,8}... | collective-permute-start | bytes 196616 | tf_op jit(solution)/shard_map/ppermute | solution.py:240
  13.4 0.0 collective-permute-done.refs_1_
  13.4 0.3 collective-permute-start.5
  13.7 0.0 collective-permute-done.1.refs_2_
  13.7 1.2 %collective-permute-start.6 = (bf16[32,1024]{1,0:T(8,128)(2,1)S(1)}, bf16[32,1024]{1,0:T(8,128)(2,1)S(1)}, u32[]{:S(2)}, u32[]{:S(2)}) collective-permute-start(bf16[32,1024]{1,0:T(8,128)(2,1)S(1)} %get-tuple-element.23), channel_id=1, source_target_pairs={{0,9},{2,11},{4,13},{6,15},{9,0},{11,2},{13,4},{15,6},{1,8},{3,10}... | collective-permute-start | bytes 196616 | tf_op jit(solution)/shard_map/ppermute | solution.py:240
  14.9 0.4 %collective-permute-done.2.refs_3_ = bf16[32,1024]{1,0:T(8,128)(2,1)S(1)} collective-permute-done((bf16[32,1024]{1,0:T(8,128)(2,1)S(1)}, bf16[32,1024]{1,0:T(8,128)(2,1)S(1)}, u32[]{:S(2)}, u32[]{:S(2)}) %collective-permute-start.2) | collective-permute-done | bytes 65568 | tf_op jit(solution)/shard_map/ppermute | solution.py:240
  15.3 0.0 collective-permute-done.3.refs_4_
  15.3 2.1 %collective-permute-done.4.refs_5_ = bf16[32,1024]{1,0:T(8,128)(2,1)S(1)} collective-permute-done((bf16[32,1024]{1,0:T(8,128)(2,1)S(1)}, bf16[32,1024]{1,0:T(8,128)(2,1)S(1)}, u32[]{:S(2)}, u32[]{:S(2)}) %collective-permute-start.4) | collective-permute-done | bytes 65568 | tf_op jit(solution)/shard_map/ppermute | solution.py:240
  17.4 2.9 %collective-permute-done.5.refs_6_ = bf16[32,1024]{1,0:T(8,128)(2,1)S(1)} collective-permute-done((bf16[32,1024]{1,0:T(8,128)(2,1)S(1)}, bf16[32,1024]{1,0:T(8,128)(2,1)S(1)}, u32[]{:S(2)}, u32[]{:S(2)}) %collective-permute-start.5) | collective-permute-done | bytes 65568 | tf_op jit(solution)/shard_map/ppermute | solution.py:240
  20.2 0.0 collective-permute-done.6.refs_7_
  20.3 0.3 %collective-permute-start.7 = (bf16[256,1024]{1,0:T(8,128)(2,1)S(1)}, bf16[256,1024]{1,0:T(8,128)(2,1)S(1)}, u32[]{:S(2)}, u32[]{:S(2)}) collective-permute-start(bf16[256,1024]{1,0:T(8,128)(2,1)S(1)} %join.1.mine_ref), channel_id=1, source_target_pairs={{0,1},{1,0},{2,3},{3,2},{4,5},{5,4},{6,7},{7,6},{8,9},{9,8},{10,11... | collective-permute-start | bytes 1572872 | tf_op jit(solution)/shard_map/ppermute | solution.py:251
  20.6 0.4 %inner.1 = (f32[1,256]{1,0:T(1,128)S(1)}, bf16[1024,256]{1,0:T(8,128)(2,1)S(1)}) custom-call(bf16[256,1024]{1,0:T(8,128)(2,1)S(1)} %join.1.mine_ref), custom_call_target="tpu_custom_call" | custom-call | tf_op jit(solution)/shard_map/inner/pallas_call | solution.py:171
  21.0 1.2 %collective-permute-done.7.other_ref = bf16[256,1024]{1,0:T(8,128)(2,1)S(1)} collective-permute-done((bf16[256,1024]{1,0:T(8,128)(2,1)S(1)}, bf16[256,1024]{1,0:T(8,128)(2,1)S(1)}, u32[]{:S(2)}, u32[]{:S(2)}) %collective-permute-start.7) | collective-permute-done | bytes 524320 | tf_op jit(solution)/shard_map/ppermute | solution.py:251
  22.3 0.4 %score.1 = f32[8,1,128]{2,1,0:T(1,128)S(1)} custom-call(s32[1]{0:T(128)} %bitcast.me_ref, f32[1,256]{1,0:T(1,128)S(1)} %get-tuple-element.24.best_ref, bf16[1024,256]{1,0:T(8,128)(2,1)S(1)} %get-tuple-element.25.turned_ref, bf16[256,1024]{1,0:T(8,128)(2,1)S(1)} %collective-permute-done.7.other_ref), custom_call_target="tpu_custom_call" | custom-call | tf_op jit(solution)/shard_map/score/pallas_call | solution.py:201
  22.6 8.7 %all_to_all.5.returned_ref = f32[8,1,128]{2,1,0:T(1,128)S(1)} all-to-all(f32[8,1,128]{2,1,0:T(1,128)S(1)} %score.1), channel_id=1, replica_groups={{0,2,4,6,9,11,13,15},{1,3,5,7,8,10,12,14},{16,18,20,22,25,27,29,31},{17..., dimensions={0} | all-to-all | bytes 8192 | tf_op jit(solution)/shard_map/all_to_all | solution.py:245
  31.4 0.6 %pick.1 = f32[1,128]{1,0:T(1,128)} custom-call(f32[8,1,128]{2,1,0:T(1,128)S(1)} %all_to_all.5.returned_ref, s32[8,128]{1,0:T(8,128)S(1)} %get-tuple-element.26.place_ref), custom_call_target="tpu_custom_call" | custom-call | tf_op jit(solution)/shard_map/pick/pallas_call | solution.py:224
  (1 shorter events, 0.0 us)
Async XLA Ops:
  2.6 10.8 %collective-permute-start = (bf16[32,1024]{1,0:T(8,128)(2,1)S(1)}, bf16[32,1024]{1,0:T(8,128)(2,1)S(1)}, u32[]{:S(2)}, u32[]{:S(2)}) collective-permute-start(bf16[32,1024]{1,0:T(8,128)(2,1)S(1)} %get-tuple-element.17), channel_id=1, source_target_pairs={{0,13},{2,15},{4,9},{6,11},{9,4},{11,6},{13,0},{15,2},{1,12},{3,14... | collective-permute-start | bytes 196616 | tf_op jit(solution)/shard_map/ppermute | solution.py:240
  7.2 6.5 %collective-permute-start.1 = (bf16[32,1024]{1,0:T(8,128)(2,1)S(1)}, bf16[32,1024]{1,0:T(8,128)(2,1)S(1)}, u32[]{:S(2)}, u32[]{:S(2)}) collective-permute-start(bf16[32,1024]{1,0:T(8,128)(2,1)S(1)} %get-tuple-element.18), channel_id=1, source_target_pairs={{0,2},{2,0},{4,6},{6,4},{9,11},{11,9},{13,15},{15,13},{1,3},{3,1},... | collective-permute-start | bytes 196616 | tf_op jit(solution)/shard_map/ppermute | solution.py:240
  8.7 6.6 %collective-permute-start.2 = (bf16[32,1024]{1,0:T(8,128)(2,1)S(1)}, bf16[32,1024]{1,0:T(8,128)(2,1)S(1)}, u32[]{:S(2)}, u32[]{:S(2)}) collective-permute-start(bf16[32,1024]{1,0:T(8,128)(2,1)S(1)} %get-tuple-element.19), channel_id=1, source_target_pairs={{0,15},{2,13},{4,11},{6,9},{9,6},{11,4},{13,2},{15,0},{1,14},{3,12... | collective-permute-start | bytes 196616 | tf_op jit(solution)/shard_map/ppermute | solution.py:240
  8.7 6.6 %collective-permute-start.3 = (bf16[32,1024]{1,0:T(8,128)(2,1)S(1)}, bf16[32,1024]{1,0:T(8,128)(2,1)S(1)}, u32[]{:S(2)}, u32[]{:S(2)}) collective-permute-start(bf16[32,1024]{1,0:T(8,128)(2,1)S(1)} %get-tuple-element.20), channel_id=1, source_target_pairs={{0,4},{2,6},{4,0},{6,2},{9,13},{11,15},{13,9},{15,11},{1,5},{3,7},... | collective-permute-start | bytes 196616 | tf_op jit(solution)/shard_map/ppermute | solution.py:240
  8.7 8.7 %collective-permute-start.4 = (bf16[32,1024]{1,0:T(8,128)(2,1)S(1)}, bf16[32,1024]{1,0:T(8,128)(2,1)S(1)}, u32[]{:S(2)}, u32[]{:S(2)}) collective-permute-start(bf16[32,1024]{1,0:T(8,128)(2,1)S(1)} %get-tuple-element.21), channel_id=1, source_target_pairs={{0,11},{2,9},{4,15},{6,13},{9,2},{11,0},{13,6},{15,4},{1,10},{3,8}... | collective-permute-start | bytes 196616 | tf_op jit(solution)/shard_map/ppermute | solution.py:240
  13.4 6.8 %collective-permute-start.5 = (bf16[32,1024]{1,0:T(8,128)(2,1)S(1)}, bf16[32,1024]{1,0:T(8,128)(2,1)S(1)}, u32[]{:S(2)}, u32[]{:S(2)}) collective-permute-start(bf16[32,1024]{1,0:T(8,128)(2,1)S(1)} %get-tuple-element.22), channel_id=1, source_target_pairs={{0,6},{2,4},{4,2},{6,0},{9,15},{11,13},{13,11},{15,9},{1,7},{3,5},... | collective-permute-start | bytes 196616 | tf_op jit(solution)/shard_map/ppermute | solution.py:240
  13.7 6.5 %collective-permute-start.6 = (bf16[32,1024]{1,0:T(8,128)(2,1)S(1)}, bf16[32,1024]{1,0:T(8,128)(2,1)S(1)}, u32[]{:S(2)}, u32[]{:S(2)}) collective-permute-start(bf16[32,1024]{1,0:T(8,128)(2,1)S(1)} %get-tuple-element.23), channel_id=1, source_target_pairs={{0,9},{2,11},{4,13},{6,15},{9,0},{11,2},{13,4},{15,6},{1,8},{3,10}... | collective-permute-start | bytes 196616 | tf_op jit(solution)/shard_map/ppermute | solution.py:240
  20.3 2.0 %collective-permute-start.7 = (bf16[256,1024]{1,0:T(8,128)(2,1)S(1)}, bf16[256,1024]{1,0:T(8,128)(2,1)S(1)}, u32[]{:S(2)}, u32[]{:S(2)}) collective-permute-start(bf16[256,1024]{1,0:T(8,128)(2,1)S(1)} %join.1.mine_ref), channel_id=1, source_target_pairs={{0,1},{1,0},{2,3},{3,2},{4,5},{5,4},{6,7},{7,6},{8,9},{9,8},{10,11... | collective-permute-start | bytes 1572872 | tf_op jit(solution)/shard_map/ppermute | solution.py:251

commit v7 on v6

--- a/solution.py
+++ b/solution.py
@@ -64,8 +64,8 @@
     earlier = (column(owner) == owner) & (iota((rows, rows), 0) < iota((rows, rows), 1))
     rank = jnp.sum(earlier.astype(jnp.int32), axis=0, keepdims=True)
     place_ref[0:1, :] = owner
-    place_ref[1:2, :] = rank
-    block = block_of(owner, me_ref[0])
+    block, spot = block_of(owner, me_ref[0])
+    place_ref[2:3, :] = spot * slot_cap + rank
     chooser = iota((slots, rows), 0) == block * slot_cap + rank
     chooser = jnp.where(chooser, 1.0, 0.0)
     empty = jnp.sum(chooser, axis=1, keepdims=True) < 0.5
@@ -97,11 +97,11 @@
     block = jnp.zeros_like(step)
     for at, other in enumerate(ORDER, 1):
         block = jnp.where(step == other, at, block)
-    return block
-
-
-def owner_block(owner, _):
-    return owner
+    return block, block
+
+
+def owner_block(owner, me):
+    return owner, me
 
 
 def embed(me, arrays, sizes, slot_cap, block_of):
@@ -181,40 +181,39 @@
     )(mine)
 
 
-def score_kernel(slot_cap, sources_of, me_ref, best_ref, turned_ref, other_ref, out_ref):
+def score_kernel(best_ref, turned_ref, other_ref, out_ref):
     scores = jnp.dot(other_ref[...], turned_ref[...], preferred_element_type=jnp.float32)
     maxima = jnp.maximum(best_ref[...], best_of(scores, other_ref))
-    for at, source in enumerate(sources_of(out_ref.shape[0], me_ref[0])):
-        out_ref[source, :, 0:slot_cap] = maxima[:, at * slot_cap : (at + 1) * slot_cap]
-
-
-def order_sources(owners, me):
-    return [me] + [me ^ step for step in ORDER]
-
-
-def owner_sources(owners, _):
-    return range(owners)
-
-
-def score(me, mine, other, owners, slot_cap, sources_of):
-    lanes = -(-slot_cap // LANES) * LANES
-    return pl.pallas_call(
-        functools.partial(score_kernel, slot_cap, sources_of),
-        out_shape=jax.ShapeDtypeStruct((owners, 1, lanes), jnp.float32),
-        in_specs=[SMEM] + [VMEM] * 3,
+    for source in range(out_ref.shape[0]):
+        out_ref[source] = maxima
+
+
+def score(mine, other, owners):
+    return pl.pallas_call(
+        score_kernel,
+        out_shape=jax.ShapeDtypeStruct((owners, 1, mine.shape[0]), jnp.float32),
+        in_specs=[VMEM] * 3,
         out_specs=VMEM,
         compiler_params=PARAMS,
         name="score",
-    )(me, *inner_best(mine), other)
+    )(*inner_best(mine), other)
 
 
 def pick_kernel(returned_ref, place_ref, out_ref):
     owners, _, lanes = returned_ref.shape
     rows = place_ref.shape[1]
     owner = place_ref[0:1, :]
-    rank = jnp.broadcast_to(place_ref[1:2, :], (owners, rows))
+    slot = jnp.broadcast_to(place_ref[2:3, :], (owners, rows))
     returned = returned_ref[...].reshape(owners, lanes)
-    taken = jnp.take_along_axis(returned, rank, axis=1, mode="promise_in_bounds")
+    taken = jnp.full((owners, rows), -3.0)
+    for start in range(0, lanes, rows):
+        part = slot - start
+        inside = (part >= 0) & (part < rows)
+        part = jnp.where(inside, part, 0)
+        found = jnp.take_along_axis(
+            returned[:, start : start + rows], part, axis=1, mode="promise_in_bounds"
+        )
+        taken = jnp.where(inside, found, taken)
     taken = jnp.where(iota((owners, rows), 0) == owner, taken, -3.0)
     out_ref[...] = jnp.max(taken, axis=0, keepdims=True)
 
@@ -256,14 +255,14 @@
     slot_cap = 2 * arrays[0].shape[0] // owners
     me = lax.axis_index("docs").reshape(1)
     if owners == len(ORDER) + 1:
-        block_of, sources_of = order_block, order_sources
+        block_of = order_block
         own, *blocks, place = embed(me, arrays, [slot_cap] * owners, slot_cap, block_of)
         mine = join([own] + [step_to(*send) for send in zip(blocks, ORDER)])
     else:
-        block_of, sources_of = owner_block, owner_sources
+        block_of = owner_block
         packed, place = embed(me, arrays, [owners * slot_cap], slot_cap, block_of)
         mine = exchange(packed)
-    maxima = score(me, mine, swap(mine), owners, slot_cap, sources_of)
+    maxima = score(mine, swap(mine), owners)
     returned = exchange(maxima)
     return pick(returned, place)
 

time: 32.1 us -> 32.1 us (level)
  no operation moved by 1% of the time
where the time goes in v7:
time: 32.1 us; the launch traced here: 32 us
  starting transfers between devices  12.6 us (39%)
  blocking collectives  8.78 us (27%)
  waiting for transfers between devices  6.58 us (20%)
  Pallas kernels  3.98 us (12%)
    ppermute x7, starting transfers between devices, step_to(): return lax.ppermute(value, ('docs', 'help'), pairs)  12.3 us
    all_to_all x1, blocking collectives, exchange(): lax.all_to_all(value, ('docs', 'help'), split_axis=0, concat_axis=0, tile...  8.78 us
    ppermute x7, waiting for transfers between devices, step_to(): return lax.ppermute(value, ('docs', 'help'), pairs)  5.34 us
    pallas_call x1, Pallas kernels, embed(): pl.pallas_call(functools.partial(embed_kernel, slot_cap, block_of), out_s...  2.61 us
    ppermute x1, waiting for transfers between devices, swap(): lax.ppermute(value, 'help', [(i, i ^ 1) for i in range(lax.axis_size('hel...  1.24 us
  transfers between devices with their start and end apart: 8, of which 4 were waited for; matrix products, arithmetic and copies ran while one was open for 0% of the time, Pallas kernels for 1%

profile of v7, /device:TPU:0, one launch (start us, length us, event | category | flops | bytes accessed | tf_op | source)
XLA Modules:
  0.0 32.0 jit_solution(13828029999110286995)
XLA Ops:
  0.0 2.6 %embed.1 = (bf16[32,1024]{1,0:T(8,128)(2,1)S(1)}, bf16[32,1024]{1,0:T(8,128)(2,1)S(1)}, bf16[32,1024]{1,0:T(8,128)(2,1)S(1)}, bf16[32,1024]{1,0:T(8,128)(2,1)S(1...) custom-call(s32[1]{0:T(128)} %bitcast.me_ref, ...), custom_call_target="tpu_custom_call" | custom-call | tf_op jit(solution)/shard_map/embed/pallas_call | solution.py:110
  2.6 4.6 %collective-permute-start = (bf16[32,1024]{1,0:T(8,128)(2,1)S(1)}, bf16[32,1024]{1,0:T(8,128)(2,1)S(1)}, u32[]{:S(2)}, u32[]{:S(2)}) collective-permute-start(bf16[32,1024]{1,0:T(8,128)(2,1)S(1)} %get-tuple-element.17), channel_id=1, source_target_pairs={{0,13},{2,15},{4,9},{6,11},{9,4},{11,6},{13,0},{15,2},{1,12},{3,14... | collective-permute-start | bytes 196616 | tf_op jit(solution)/shard_map/ppermute | solution.py:239
  7.2 1.5 %collective-permute-start.1 = (bf16[32,1024]{1,0:T(8,128)(2,1)S(1)}, bf16[32,1024]{1,0:T(8,128)(2,1)S(1)}, u32[]{:S(2)}, u32[]{:S(2)}) collective-permute-start(bf16[32,1024]{1,0:T(8,128)(2,1)S(1)} %get-tuple-element.18), channel_id=1, source_target_pairs={{0,2},{2,0},{4,6},{6,4},{9,11},{11,9},{13,15},{15,13},{1,3},{3,1},... | collective-permute-start | bytes 196616 | tf_op jit(solution)/shard_map/ppermute | solution.py:239
  8.7 0.0 collective-permute-start.2
  8.7 0.0 collective-permute-start.3
  8.7 4.7 %collective-permute-start.4 = (bf16[32,1024]{1,0:T(8,128)(2,1)S(1)}, bf16[32,1024]{1,0:T(8,128)(2,1)S(1)}, u32[]{:S(2)}, u32[]{:S(2)}) collective-permute-start(bf16[32,1024]{1,0:T(8,128)(2,1)S(1)} %get-tuple-element.21), channel_id=1, source_target_pairs={{0,11},{2,9},{4,15},{6,13},{9,2},{11,0},{13,6},{15,4},{1,10},{3,8}... | collective-permute-start | bytes 196616 | tf_op jit(solution)/shard_map/ppermute | solution.py:239
  13.4 0.0 collective-permute-done.refs_1_
  13.4 0.3 collective-permute-start.5
  13.7 0.0 collective-permute-done.1.refs_2_
  13.7 1.2 %collective-permute-start.6 = (bf16[32,1024]{1,0:T(8,128)(2,1)S(1)}, bf16[32,1024]{1,0:T(8,128)(2,1)S(1)}, u32[]{:S(2)}, u32[]{:S(2)}) collective-permute-start(bf16[32,1024]{1,0:T(8,128)(2,1)S(1)} %get-tuple-element.23), channel_id=1, source_target_pairs={{0,9},{2,11},{4,13},{6,15},{9,0},{11,2},{13,4},{15,6},{1,8},{3,10}... | collective-permute-start | bytes 196616 | tf_op jit(solution)/shard_map/ppermute | solution.py:239
  14.9 0.4 %collective-permute-done.2.refs_3_ = bf16[32,1024]{1,0:T(8,128)(2,1)S(1)} collective-permute-done((bf16[32,1024]{1,0:T(8,128)(2,1)S(1)}, bf16[32,1024]{1,0:T(8,128)(2,1)S(1)}, u32[]{:S(2)}, u32[]{:S(2)}) %collective-permute-start.2) | collective-permute-done | bytes 65568 | tf_op jit(solution)/shard_map/ppermute | solution.py:239
  15.3 0.0 collective-permute-done.3.refs_4_
  15.3 2.1 %collective-permute-done.4.refs_5_ = bf16[32,1024]{1,0:T(8,128)(2,1)S(1)} collective-permute-done((bf16[32,1024]{1,0:T(8,128)(2,1)S(1)}, bf16[32,1024]{1,0:T(8,128)(2,1)S(1)}, u32[]{:S(2)}, u32[]{:S(2)}) %collective-permute-start.4) | collective-permute-done | bytes 65568 | tf_op jit(solution)/shard_map/ppermute | solution.py:239
  17.4 2.9 %collective-permute-done.5.refs_6_ = bf16[32,1024]{1,0:T(8,128)(2,1)S(1)} collective-permute-done((bf16[32,1024]{1,0:T(8,128)(2,1)S(1)}, bf16[32,1024]{1,0:T(8,128)(2,1)S(1)}, u32[]{:S(2)}, u32[]{:S(2)}) %collective-permute-start.5) | collective-permute-done | bytes 65568 | tf_op jit(solution)/shard_map/ppermute | solution.py:239
  20.2 0.0 collective-permute-done.6.refs_7_
  20.3 0.3 %collective-permute-start.7 = (bf16[256,1024]{1,0:T(8,128)(2,1)S(1)}, bf16[256,1024]{1,0:T(8,128)(2,1)S(1)}, u32[]{:S(2)}, u32[]{:S(2)}) collective-permute-start(bf16[256,1024]{1,0:T(8,128)(2,1)S(1)} %join.1.mine_ref), channel_id=1, source_target_pairs={{0,1},{1,0},{2,3},{3,2},{4,5},{5,4},{6,7},{7,6},{8,9},{9,8},{10,11... | collective-permute-start | bytes 1572872 | tf_op jit(solution)/shard_map/ppermute | solution.py:250
  20.6 0.4 %inner.1 = (f32[1,256]{1,0:T(1,128)S(1)}, bf16[1024,256]{1,0:T(8,128)(2,1)S(1)}) custom-call(bf16[256,1024]{1,0:T(8,128)(2,1)S(1)} %join.1.mine_ref), custom_call_target="tpu_custom_call" | custom-call | tf_op jit(solution)/shard_map/inner/pallas_call | solution.py:171
  21.0 1.2 %collective-permute-done.7.other_ref = bf16[256,1024]{1,0:T(8,128)(2,1)S(1)} collective-permute-done((bf16[256,1024]{1,0:T(8,128)(2,1)S(1)}, bf16[256,1024]{1,0:T(8,128)(2,1)S(1)}, u32[]{:S(2)}, u32[]{:S(2)}) %collective-permute-start.7) | collective-permute-done | bytes 524320 | tf_op jit(solution)/shard_map/ppermute | solution.py:250
  22.3 0.3 score.1
  22.6 8.8 %all_to_all.5.returned_ref = f32[8,1,256]{2,1,0:T(1,128)S(1)} all-to-all(f32[8,1,256]{2,1,0:T(1,128)S(1)} %score.1), channel_id=1, replica_groups={{0,2,4,6,9,11,13,15},{1,3,5,7,8,10,12,14},{16,18,20,22,25,27,29,31},{17..., dimensions={0} | all-to-all | bytes 16384 | tf_op jit(solution)/shard_map/all_to_all | solution.py:244
  31.4 0.6 %pick.1 = f32[1,128]{1,0:T(1,128)} custom-call(f32[8,1,256]{2,1,0:T(1,128)S(1)} %all_to_all.5.returned_ref, s32[8,128]{1,0:T(8,128)S(1)} %get-tuple-element.26.place_ref), custom_call_target="tpu_custom_call" | custom-call | tf_op jit(solution)/shard_map/pick/pallas_call | solution.py:223
  (1 shorter events, 0.0 us)
Async XLA Ops:
  2.6 10.8 %collective-permute-start = (bf16[32,1024]{1,0:T(8,128)(2,1)S(1)}, bf16[32,1024]{1,0:T(8,128)(2,1)S(1)}, u32[]{:S(2)}, u32[]{:S(2)}) collective-permute-start(bf16[32,1024]{1,0:T(8,128)(2,1)S(1)} %get-tuple-element.17), channel_id=1, source_target_pairs={{0,13},{2,15},{4,9},{6,11},{9,4},{11,6},{13,0},{15,2},{1,12},{3,14... | collective-permute-start | bytes 196616 | tf_op jit(solution)/shard_map/ppermute | solution.py:239
  7.2 6.5 %collective-permute-start.1 = (bf16[32,1024]{1,0:T(8,128)(2,1)S(1)}, bf16[32,1024]{1,0:T(8,128)(2,1)S(1)}, u32[]{:S(2)}, u32[]{:S(2)}) collective-permute-start(bf16[32,1024]{1,0:T(8,128)(2,1)S(1)} %get-tuple-element.18), channel_id=1, source_target_pairs={{0,2},{2,0},{4,6},{6,4},{9,11},{11,9},{13,15},{15,13},{1,3},{3,1},... | collective-permute-start | bytes 196616 | tf_op jit(solution)/shard_map/ppermute | solution.py:239
  8.7 6.6 %collective-permute-start.2 = (bf16[32,1024]{1,0:T(8,128)(2,1)S(1)}, bf16[32,1024]{1,0:T(8,128)(2,1)S(1)}, u32[]{:S(2)}, u32[]{:S(2)}) collective-permute-start(bf16[32,1024]{1,0:T(8,128)(2,1)S(1)} %get-tuple-element.19), channel_id=1, source_target_pairs={{0,15},{2,13},{4,11},{6,9},{9,6},{11,4},{13,2},{15,0},{1,14},{3,12... | collective-permute-start | bytes 196616 | tf_op jit(solution)/shard_map/ppermute | solution.py:239
  8.7 6.6 %collective-permute-start.3 = (bf16[32,1024]{1,0:T(8,128)(2,1)S(1)}, bf16[32,1024]{1,0:T(8,128)(2,1)S(1)}, u32[]{:S(2)}, u32[]{:S(2)}) collective-permute-start(bf16[32,1024]{1,0:T(8,128)(2,1)S(1)} %get-tuple-element.20), channel_id=1, source_target_pairs={{0,4},{2,6},{4,0},{6,2},{9,13},{11,15},{13,9},{15,11},{1,5},{3,7},... | collective-permute-start | bytes 196616 | tf_op jit(solution)/shard_map/ppermute | solution.py:239
  8.7 8.7 %collective-permute-start.4 = (bf16[32,1024]{1,0:T(8,128)(2,1)S(1)}, bf16[32,1024]{1,0:T(8,128)(2,1)S(1)}, u32[]{:S(2)}, u32[]{:S(2)}) collective-permute-start(bf16[32,1024]{1,0:T(8,128)(2,1)S(1)} %get-tuple-element.21), channel_id=1, source_target_pairs={{0,11},{2,9},{4,15},{6,13},{9,2},{11,0},{13,6},{15,4},{1,10},{3,8}... | collective-permute-start | bytes 196616 | tf_op jit(solution)/shard_map/ppermute | solution.py:239
  13.4 6.8 %collective-permute-start.5 = (bf16[32,1024]{1,0:T(8,128)(2,1)S(1)}, bf16[32,1024]{1,0:T(8,128)(2,1)S(1)}, u32[]{:S(2)}, u32[]{:S(2)}) collective-permute-start(bf16[32,1024]{1,0:T(8,128)(2,1)S(1)} %get-tuple-element.22), channel_id=1, source_target_pairs={{0,6},{2,4},{4,2},{6,0},{9,15},{11,13},{13,11},{15,9},{1,7},{3,5},... | collective-permute-start | bytes 196616 | tf_op jit(solution)/shard_map/ppermute | solution.py:239
  13.7 6.5 %collective-permute-start.6 = (bf16[32,1024]{1,0:T(8,128)(2,1)S(1)}, bf16[32,1024]{1,0:T(8,128)(2,1)S(1)}, u32[]{:S(2)}, u32[]{:S(2)}) collective-permute-start(bf16[32,1024]{1,0:T(8,128)(2,1)S(1)} %get-tuple-element.23), channel_id=1, source_target_pairs={{0,9},{2,11},{4,13},{6,15},{9,0},{11,2},{13,4},{15,6},{1,8},{3,10}... | collective-permute-start | bytes 196616 | tf_op jit(solution)/shard_map/ppermute | solution.py:239
  20.3 2.0 %collective-permute-start.7 = (bf16[256,1024]{1,0:T(8,128)(2,1)S(1)}, bf16[256,1024]{1,0:T(8,128)(2,1)S(1)}, u32[]{:S(2)}, u32[]{:S(2)}) collective-permute-start(bf16[256,1024]{1,0:T(8,128)(2,1)S(1)} %join.1.mine_ref), channel_id=1, source_target_pairs={{0,1},{1,0},{2,3},{3,2},{4,5},{5,4},{6,7},{7,6},{8,9},{9,8},{10,11... | collective-permute-start | bytes 1572872 | tf_op jit(solution)/shard_map/ppermute | solution.py:250
